TPU v7x, 512 devices: a whole 4x8x8 slice. The times are simulated.
512 devices in a mesh: group: 16 (over z_lo, x, core), blk: 32 (over y, z_hi).
Axes of the slice: x: 4, y: 8, z: 8 (z_hi: 4, z_lo: 2; z = z_hi * 2 + z_lo), core: 2. Of those that a mesh axis runs over, the one named last changes fastest.
Arguments:
- pre_img: bfloat16 [196608, 768], P(('group', 'blk')), may hold values from -6 to 6
- pre_txt: bfloat16 [196608, 768], P(('group', 'blk')), may hold values from -6 to 6
Outputs:
- grad_img: float32 [196608, 768], P(('group', 'blk'))
- grad_txt: float32 [196608, 768], P(('group', 'blk'))
- row_loss: float32 [196608], P(('group', 'blk'))
All inputs are finite; a program needn't handle non-finite values.
Results may differ from a plain program's by a relative error of at most 0.0069.
Values may be sent and summed in bfloat16 or wider, within the bound.
No kernel may reach another device: no remote copies, remote signals or barrier semaphores. Data moves between devices by JAX's collectives and lax.ppermute only.
A program may use at most 64 MiB of HBM per device.

v0:
```python
import jax
import jax.numpy as jnp
from jax import lax
from jax.sharding import PartitionSpec as P

HOPS = 4


logit_scale = 0.32


def shifted(array, axis, by):
    peers = lax.axis_size(axis)
    return lax.ppermute(array, axis, [(i, (i + by) % peers) for i in range(peers)])


def block_scores(row_block, col_block):
    return logit_scale * jnp.einsum(
        "re,ce->rc", row_block, col_block, preferred_element_type=jnp.float32
    )


def block_parts(scores):
    peak_value = jnp.max(scores, axis=1)
    row_total = jnp.sum(jnp.exp(scores - peak_value[:, None]), axis=1)
    return (peak_value, row_total)


def combine_parts(first, second):
    peak_value = jnp.maximum(first[0], second[0])
    row_total = first[1] * jnp.exp(first[0] - peak_value) + second[1] * jnp.exp(
        second[0] - peak_value
    )
    return (peak_value, row_total)


def weights_of(scores, log_total, diag_mask):
    return (jnp.exp(scores - log_total[:, None]) - diag_mask).astype(jnp.bfloat16)


def row_term(weights, col_block):
    return logit_scale * jnp.dot(weights, col_block, preferred_element_type=jnp.float32)


def col_term(weights, row_block):
    return logit_scale * jnp.einsum(
        "rc,re->ce", weights, row_block, preferred_element_type=jnp.float32
    )


def per_device(pre_img, pre_txt):
    img_soft = jnp.tanh(pre_img.astype(jnp.float32))
    txt_soft = jnp.tanh(pre_txt.astype(jnp.float32))
    images = img_soft.astype(jnp.bfloat16)
    texts = txt_soft.astype(jnp.bfloat16)
    row_count = images.shape[0]
    eye_mask = (
        lax.broadcasted_iota(jnp.int32, (row_count, row_count), 0)
        == lax.broadcasted_iota(jnp.int32, (row_count, row_count), 1)
    ).astype(jnp.float32)
    blocks = [texts]
    moving = texts
    for offset in range(HOPS):
        moving = shifted(moving, "blk", 1)
        blocks.append(moving)
    score_list = []
    for position in range(HOPS + 1):
        score_list.append(block_scores(images, blocks[position]))
    partial_value = block_parts(score_list[0])
    for position in range(1, HOPS + 1):
        partial_value = combine_parts(partial_value, block_parts(score_list[position]))
    hop_block = shifted(texts, "group", 1)
    hop_scores = block_scores(images, hop_block)
    partial_value = combine_parts(partial_value, block_parts(hop_scores))
    log_total = partial_value[0] + jnp.log(partial_value[1])
    row_loss = log_total - jnp.sum(score_list[0] * eye_mask, axis=1)
    row_grad = jnp.zeros(images.shape, jnp.float32)
    text_terms = []
    for position in range(HOPS + 1):
        diag_mask = eye_mask if position == 0 else 0.0
        weights = weights_of(score_list[position], log_total, diag_mask)
        row_grad = row_grad + row_term(weights, blocks[position])
        text_terms.append(col_term(weights, images))
    text_grad = text_terms[HOPS]
    for offset in range(HOPS - 1, -1, -1):
        text_grad = (
            shifted(text_grad.astype(jnp.bfloat16), "blk", -1).astype(text_grad.dtype)
            + text_terms[offset]
        )
    weights = weights_of(hop_scores, log_total, 0.0)
    row_grad = row_grad + row_term(weights, hop_block)
    text_grad = text_grad + shifted(
        col_term(weights, images).astype(jnp.bfloat16), "group", -1
    ).astype(jnp.float32)
    grad_img = row_grad * (1.0 - img_soft * img_soft)
    grad_txt = text_grad * (1.0 - txt_soft * txt_soft)
    return (grad_img, grad_txt, row_loss)


def solution(mesh):
    in_specs = (P(("group", "blk"), None), P(("group", "blk"), None))
    out_specs = (P(("group", "blk"), None), P(("group", "blk"), None), P(("group", "blk")))
    return jax.shard_map(
        per_device, mesh=mesh, in_specs=in_specs, out_specs=out_specs, check_vma=False
    )
```

profile of v0, /device:TPU:6, one launch (start us, length us, event | category | flops | bytes accessed | tf_op | source)
XLA Modules:
  0.0 267.7 jit_solution(11239099617156588423)
XLA Ops:
  0.6 1.3 fusion.5
  2.0 6.1 %collective-permute-start = (bf16[384,768]{1,0:T(8,128)(2,1)S(1)}, bf16[384,768]{1,0:T(8,128)(2,1)S(1)}, u32[]{:S(2)}, u32[]{:S(2)}) collective-permute-start(bf16[384,768]{1,0:T(8,128)(2,1)S(1)} %fusion.5), channel_id=1, source_target_pairs={{0,1},{1,2},{2,3},{3,4},{4,5},{5,6},{6,7},{7,8},{8,9},{9,10},{10,1... | collective-permute-start | bytes 1769480 | tf_op jit(solution)/shard_map/ppermute | solution.py:14
  8.1 33.7 %collective-permute-done = bf16[384,768]{1,0:T(8,128)(2,1)S(1)} collective-permute-done((bf16[384,768]{1,0:T(8,128)(2,1)S(1)}, bf16[384,768]{1,0:T(8,128)(2,1)S(1)}, u32[]{:S(2)}, u32[]{:S(2)}) %collective-permute-start) | collective-permute-done | bytes 589856 | tf_op jit(solution)/shard_map/ppermute | solution.py:14
  41.8 1.9 collective-permute-start.1
  43.7 1.9 collective-permute-start.4
  46.3 28.1 %collective-permute-done.1 = bf16[384,768]{1,0:T(8,128)(2,1)S(1)} collective-permute-done((bf16[384,768]{1,0:T(8,128)(2,1)S(1)}, bf16[384,768]{1,0:T(8,128)(2,1)S(1)}, u32[]{:S(2)}, u32[]{:S(2)}) %collective-permute-start.1) | collective-permute-done | bytes 589856 | tf_op jit(solution)/shard_map/ppermute | solution.py:14
  74.4 1.9 collective-permute-start.2
  77.6 24.2 %collective-permute-done.2 = bf16[384,768]{1,0:T(8,128)(2,1)S(1)} collective-permute-done((bf16[384,768]{1,0:T(8,128)(2,1)S(1)}, bf16[384,768]{1,0:T(8,128)(2,1)S(1)}, u32[]{:S(2)}, u32[]{:S(2)}) %collective-permute-start.2) | collective-permute-done | bytes 589856 | tf_op jit(solution)/shard_map/ppermute | solution.py:14
  101.8 1.9 collective-permute-start.3
  105.1 27.3 %collective-permute-done.3 = bf16[384,768]{1,0:T(8,128)(2,1)S(1)} collective-permute-done((bf16[384,768]{1,0:T(8,128)(2,1)S(1)}, bf16[384,768]{1,0:T(8,128)(2,1)S(1)}, u32[]{:S(2)}, u32[]{:S(2)}) %collective-permute-start.3) | collective-permute-done | bytes 589856 | tf_op jit(solution)/shard_map/ppermute | solution.py:14
  133.0 0.6 fusion.33
  133.7 0.6 fusion.8
  135.3 1.9 collective-permute-start.9
  137.2 5.4 %collective-permute-start.5 = (bf16[384,768]{1,0:T(8,128)(2,1)S(1)}, bf16[384,768]{1,0:T(8,128)(2,1)S(1)}, u32[]{:S(2)}, u32[]{:S(2)}) collective-permute-start(bf16[384,768]{1,0:T(8,128)(2,1)S(1)} %fusion.3), channel_id=1, source_target_pairs={{0,31},{1,0},{2,1},{3,2},{4,3},{5,4},{6,5},{7,6},{8,7},{9,8},{10,9... | collective-permute-start | bytes 1769480 | tf_op jit(solution)/shard_map/ppermute | solution.py:14
  143.7 28.5 %collective-permute-done.5 = bf16[384,768]{1,0:T(8,128)(2,1)S(1)} collective-permute-done((bf16[384,768]{1,0:T(8,128)(2,1)S(1)}, bf16[384,768]{1,0:T(8,128)(2,1)S(1)}, u32[]{:S(2)}, u32[]{:S(2)}) %collective-permute-start.5) | collective-permute-done | bytes 589856 | tf_op jit(solution)/shard_map/ppermute | solution.py:14
  172.2 0.5 add_convert_fusion.2
  172.7 2.7 %collective-permute-start.6 = (bf16[384,768]{1,0:T(8,128)(2,1)S(1)}, bf16[384,768]{1,0:T(8,128)(2,1)S(1)}, u32[]{:S(2)}, u32[]{:S(2)}) collective-permute-start(bf16[384,768]{1,0:T(8,128)(2,1)S(1)} %add_convert_fusion.2), channel_id=1, source_target_pairs={{0,31},{1,0},{2,1},{3,2},{4,3},{5,4},{6,5},{7,6},{8,7},{9,8},{10,9... | collective-permute-start | bytes 1769480 | tf_op jit(solution)/shard_map/ppermute | solution.py:14
  176.5 34.2 %collective-permute-done.6 = bf16[384,768]{1,0:T(8,128)(2,1)S(1)} collective-permute-done((bf16[384,768]{1,0:T(8,128)(2,1)S(1)}, bf16[384,768]{1,0:T(8,128)(2,1)S(1)}, u32[]{:S(2)}, u32[]{:S(2)}) %collective-permute-start.6) | collective-permute-done | bytes 589856 | tf_op jit(solution)/shard_map/ppermute | solution.py:14
  210.8 1.9 collective-permute-start.7
  213.8 34.3 %collective-permute-done.7 = bf16[384,768]{1,0:T(8,128)(2,1)S(1)} collective-permute-done((bf16[384,768]{1,0:T(8,128)(2,1)S(1)}, bf16[384,768]{1,0:T(8,128)(2,1)S(1)}, u32[]{:S(2)}, u32[]{:S(2)}) %collective-permute-start.7) | collective-permute-done | bytes 589856 | tf_op jit(solution)/shard_map/ppermute | solution.py:14
  248.3 1.9 collective-permute-start.8
  250.7 1.7 fusion.2
  252.4 13.9 %collective-permute-done.8 = bf16[384,768]{1,0:T(8,128)(2,1)S(1)} collective-permute-done((bf16[384,768]{1,0:T(8,128)(2,1)S(1)}, bf16[384,768]{1,0:T(8,128)(2,1)S(1)}, u32[]{:S(2)}, u32[]{:S(2)}) %collective-permute-start.8) | collective-permute-done | bytes 589856 | tf_op jit(solution)/shard_map/ppermute | solution.py:14
  266.3 1.4 subtract_multiply_fusion
  (29 shorter events, 8.9 us)
Async XLA Ops:
  0.6 45.0 %copy-start.1 = (bf16[384,768]{1,0:T(8,128)(2,1)S(1)}, bf16[384,768]{1,0:T(8,128)(2,1)}, u32[]{:S(2)}) copy-start(bf16[384,768]{1,0:T(8,128)(2,1)} %param.3) | copy-start | bytes 1769476
  0.6 45.0 %copy-start = (bf16[384,768]{1,0:T(8,128)(2,1)S(1)}, bf16[384,768]{1,0:T(8,128)(2,1)}, u32[]{:S(2)}) copy-start(bf16[384,768]{1,0:T(8,128)(2,1)} %param.2) | copy-start | bytes 1769476
  2.0 39.8 %collective-permute-start = (bf16[384,768]{1,0:T(8,128)(2,1)S(1)}, bf16[384,768]{1,0:T(8,128)(2,1)S(1)}, u32[]{:S(2)}, u32[]{:S(2)}) collective-permute-start(bf16[384,768]{1,0:T(8,128)(2,1)S(1)} %fusion.5), channel_id=1, source_target_pairs={{0,1},{1,2},{2,3},{3,4},{4,5},{5,6},{6,7},{7,8},{8,9},{9,10},{10,1... | collective-permute-start | bytes 1769480 | tf_op jit(solution)/shard_map/ppermute | solution.py:14
  41.8 32.6 %collective-permute-start.1 = (bf16[384,768]{1,0:T(8,128)(2,1)S(1)}, bf16[384,768]{1,0:T(8,128)(2,1)S(1)}, u32[]{:S(2)}, u32[]{:S(2)}) collective-permute-start(bf16[384,768]{1,0:T(8,128)(2,1)S(1)} %collective-permute-done), channel_id=1, source_target_pairs={{0,1},{1,2},{2,3},{3,4},{4,5},{5,6},{6,7},{7,8},{8,9},{9,10},{10,1... | collective-permute-start | bytes 1769480 | tf_op jit(solution)/shard_map/ppermute | solution.py:14
  43.7 32.6 %collective-permute-start.4 = (bf16[384,768]{1,0:T(8,128)(2,1)S(1)}, bf16[384,768]{1,0:T(8,128)(2,1)S(1)}, u32[]{:S(2)}, u32[]{:S(2)}) collective-permute-start(bf16[384,768]{1,0:T(8,128)(2,1)S(1)} %fusion.5), channel_id=1, source_target_pairs={{0,32},{32,64},{64,96},{96,128},{128,160},{160,192},{192,224},{224... | collective-permute-start | bytes 1769480 | tf_op jit(solution)/shard_map/ppermute | solution.py:14
  74.4 27.5 %collective-permute-start.2 = (bf16[384,768]{1,0:T(8,128)(2,1)S(1)}, bf16[384,768]{1,0:T(8,128)(2,1)S(1)}, u32[]{:S(2)}, u32[]{:S(2)}) collective-permute-start(bf16[384,768]{1,0:T(8,128)(2,1)S(1)} %collective-permute-done.1), channel_id=1, source_target_pairs={{0,1},{1,2},{2,3},{3,4},{4,5},{5,6},{6,7},{7,8},{8,9},{9,10},{10,1... | collective-permute-start | bytes 1769480 | tf_op jit(solution)/shard_map/ppermute | solution.py:14
  101.8 30.6 %collective-permute-start.3 = (bf16[384,768]{1,0:T(8,128)(2,1)S(1)}, bf16[384,768]{1,0:T(8,128)(2,1)S(1)}, u32[]{:S(2)}, u32[]{:S(2)}) collective-permute-start(bf16[384,768]{1,0:T(8,128)(2,1)S(1)} %collective-permute-done.2), channel_id=1, source_target_pairs={{0,1},{1,2},{2,3},{3,4},{4,5},{5,6},{6,7},{7,8},{8,9},{9,10},{10,1... | collective-permute-start | bytes 1769480 | tf_op jit(solution)/shard_map/ppermute | solution.py:14
  135.3 117.0 %collective-permute-start.9 = (bf16[384,768]{1,0:T(8,128)(2,1)S(1)}, bf16[384,768]{1,0:T(8,128)(2,1)S(1)}, u32[]{:S(2)}, u32[]{:S(2)}) collective-permute-start(bf16[384,768]{1,0:T(8,128)(2,1)S(1)} %fusion.4), channel_id=1, source_target_pairs={{0,480},{32,0},{64,32},{96,64},{128,96},{160,128},{192,160},{224,1... | collective-permute-start | bytes 1769480 | tf_op jit(solution)/shard_map/ppermute | solution.py:14
  137.2 34.9 %collective-permute-start.5 = (bf16[384,768]{1,0:T(8,128)(2,1)S(1)}, bf16[384,768]{1,0:T(8,128)(2,1)S(1)}, u32[]{:S(2)}, u32[]{:S(2)}) collective-permute-start(bf16[384,768]{1,0:T(8,128)(2,1)S(1)} %fusion.3), channel_id=1, source_target_pairs={{0,31},{1,0},{2,1},{3,2},{4,3},{5,4},{6,5},{7,6},{8,7},{9,8},{10,9... | collective-permute-start | bytes 1769480 | tf_op jit(solution)/shard_map/ppermute | solution.py:14
  172.7 38.0 %collective-permute-start.6 = (bf16[384,768]{1,0:T(8,128)(2,1)S(1)}, bf16[384,768]{1,0:T(8,128)(2,1)S(1)}, u32[]{:S(2)}, u32[]{:S(2)}) collective-permute-start(bf16[384,768]{1,0:T(8,128)(2,1)S(1)} %add_convert_fusion.2), channel_id=1, source_target_pairs={{0,31},{1,0},{2,1},{3,2},{4,3},{5,4},{6,5},{7,6},{8,7},{9,8},{10,9... | collective-permute-start | bytes 1769480 | tf_op jit(solution)/shard_map/ppermute | solution.py:14
  210.8 37.3 %collective-permute-start.7 = (bf16[384,768]{1,0:T(8,128)(2,1)S(1)}, bf16[384,768]{1,0:T(8,128)(2,1)S(1)}, u32[]{:S(2)}, u32[]{:S(2)}) collective-permute-start(bf16[384,768]{1,0:T(8,128)(2,1)S(1)} %add_convert_fusion.1), channel_id=1, source_target_pairs={{0,31},{1,0},{2,1},{3,2},{4,3},{5,4},{6,5},{7,6},{8,7},{9,8},{10,9... | collective-permute-start | bytes 1769480 | tf_op jit(solution)/shard_map/ppermute | solution.py:14
  248.3 18.0 %collective-permute-start.8 = (bf16[384,768]{1,0:T(8,128)(2,1)S(1)}, bf16[384,768]{1,0:T(8,128)(2,1)S(1)}, u32[]{:S(2)}, u32[]{:S(2)}) collective-permute-start(bf16[384,768]{1,0:T(8,128)(2,1)S(1)} %add_convert_fusion), channel_id=1, source_target_pairs={{0,31},{1,0},{2,1},{3,2},{4,3},{5,4},{6,5},{7,6},{8,7},{9,8},{10,9... | collective-permute-start | bytes 1769480 | tf_op jit(solution)/shard_map/ppermute | solution.py:14
where the time goes:
time: 271 us; the launch traced here: 268 us
  waiting for transfers between devices  224 us (83%)
  starting transfers between devices  27.6 us (10%)
  matrix products  10.6 us (4%)
  other arithmetic  4.3 us (2%)
    ppermute x10, waiting for transfers between devices, shifted(): lax.ppermute(array, axis, [(i, (i + by) % peers) for i in range(peers)])  224 us
    ppermute x10, starting transfers between devices, shifted(): lax.ppermute(array, axis, [(i, (i + by) % peers) for i in range(peers)])  27.6 us
  transfers between devices with their start and end apart: 10, of which 8 were waited for; matrix products, arithmetic and copies ran while one was open for 3% of the time, Pallas kernels for 0%

commit v1 on v0

v1 whole, which is shorter than its diff:
```python
import jax
import jax.numpy as jnp
from jax import lax
from jax.sharding import PartitionSpec as P

logit_scale = 0.32
AXES = ("group", "blk")
LOW = -1e30


def scores_of(rows, cols):
    return logit_scale * jnp.einsum(
        "re,ce->rc", rows, cols, preferred_element_type=jnp.float32
    )


def stats_of(scores):
    peak = jnp.max(scores, axis=1)
    return peak, jnp.sum(jnp.exp(scores - peak[:, None]), axis=1)


def merge(first, second):
    peak = jnp.maximum(first[0], second[0])
    total = first[1] * jnp.exp(first[0] - peak) + second[1] * jnp.exp(second[0] - peak)
    return peak, total


def soft(scores, offset):
    return jnp.exp(scores - offset[:, None])


def dot(weights, cols):
    return jnp.dot(
        weights.astype(jnp.bfloat16), cols, preferred_element_type=jnp.float32
    )


def dot_t(weights, rows):
    return jnp.einsum(
        "rc,re->ce", weights.astype(jnp.bfloat16), rows, preferred_element_type=jnp.float32
    )


def solution(mesh):
    groups, blks = mesh.shape["group"], mesh.shape["blk"]

    def even(g, b):
        return (g + b) % 2 == 0

    def pairs(move):
        out = []
        for g in range(groups):
            for b in range(blks):
                to_g, to_b = move(g, b)
                out.append((g * blks + b, (to_g % groups) * blks + to_b % blks))
        return out

    swap = pairs(lambda g, b: (g, b + 1 if even(g, b) else b - 1))
    cross = pairs(lambda g, b: (g, b - 1 if even(g, b) else b - 3))
    uncross = [(t, s) for s, t in cross]
    back = pairs(lambda g, b: (g, b - 4))
    forth = [(t, s) for s, t in back]
    hop = pairs(lambda g, b: (g + 1, b))
    unhop = [(t, s) for s, t in hop]

    def send(array, plan):
        return lax.ppermute(array, AXES, plan)

    def per_device(pre_img, pre_txt):
        is_even = (lax.axis_index("group") + lax.axis_index("blk")) % 2 == 0
        img_soft = jnp.tanh(pre_img.astype(jnp.float32))
        txt_soft = jnp.tanh(pre_txt.astype(jnp.float32))
        image = img_soft.astype(jnp.bfloat16)
        text = txt_soft.astype(jnp.bfloat16)
        rows = image.shape[0]
        eye = (
            lax.broadcasted_iota(jnp.int32, (rows, rows), 0)
            == lax.broadcasted_iota(jnp.int32, (rows, rows), 1)
        ).astype(jnp.float32)

        text_p = send(text, swap)
        image_x = send(image, cross)
        image_v = send(image, back)
        text_h = send(text, hop)

        s_own = scores_of(image, text)
        s_vt = scores_of(image_v, text)
        s_hop = scores_of(image, text_h)
        s_xt = scores_of(image_x, text)
        s_xp = scores_of(image_x, text_p)
        image_y = jnp.where(is_even, image_v, image)
        s_yp = scores_of(image_y, text_p)

        stat_x = merge(stats_of(s_xt), stats_of(s_xp))
        stat_y = stats_of(s_yp)
        stat_v = merge(
            stats_of(s_vt),
            (jnp.where(is_even, stat_y[0], LOW), jnp.where(is_even, stat_y[1], 0.0)),
        )
        stat_i = merge(stats_of(s_own), stats_of(s_hop))
        stat_i = merge(
            stat_i,
            (jnp.where(is_even, LOW, stat_y[0]), jnp.where(is_even, 0.0, stat_y[1])),
        )
        got_x = send(jnp.stack(stat_x), uncross)
        got_v = send(jnp.stack(stat_v), forth)

        grad_y = dot(soft(s_yp, stat_y[0]), text_p)
        part_x = dot(soft(s_xt, stat_x[0]), text) + dot(soft(s_xp, stat_x[0]), text_p)
        scale_y = jnp.where(is_even, jnp.exp(stat_y[0] - stat_v[0]), 0.0)
        part_v = dot(soft(s_vt, stat_v[0]), text) + grad_y * scale_y[:, None]
        home_x = send(part_x.astype(jnp.bfloat16), uncross)
        home_v = send(part_v.astype(jnp.bfloat16), forth)

        peak, total = merge(merge(stat_i, (got_x[0], got_x[1])), (got_v[0], got_v[1]))
        lse = peak + jnp.log(total)
        lse_x = send(lse, cross)
        lse_v = send(lse, back)
        row_loss = lse - jnp.sum(s_own * eye, axis=1)

        lse_y = jnp.where(is_even, lse_v, lse)
        w_hop = soft(s_hop, lse)
        w_own = soft(s_own, lse) - eye
        term_p = dot_t(soft(s_xp, lse_x), image_x) + dot_t(soft(s_yp, lse_y), image_y)
        got_p = send(term_p.astype(jnp.bfloat16), swap)
        got_h = send(dot_t(w_hop, image).astype(jnp.bfloat16), unhop)

        scale_o = jnp.where(is_even, 0.0, jnp.exp(jnp.minimum(stat_y[0] - lse, 0.0)))
        row_grad = (
            dot(w_own, text)
            + dot(w_hop, text_h)
            + grad_y * scale_o[:, None]
            + home_x.astype(jnp.float32) * jnp.exp(got_x[0] - lse)[:, None]
            + home_v.astype(jnp.float32) * jnp.exp(got_v[0] - lse)[:, None]
        )
        text_grad = (
            dot_t(w_own, image)
            + dot_t(soft(s_vt, lse_v), image_v)
            + dot_t(soft(s_xt, lse_x), image_x)
            + got_p.astype(jnp.float32)
            + got_h.astype(jnp.float32)
        )
        grad_img = logit_scale * row_grad * (1.0 - img_soft * img_soft)
        grad_txt = logit_scale * text_grad * (1.0 - txt_soft * txt_soft)
        return grad_img, grad_txt, row_loss

    in_specs = (P(AXES, None), P(AXES, None))
    out_specs = (P(AXES, None), P(AXES, None), P(AXES))
    return jax.shard_map(
        per_device, mesh=mesh, in_specs=in_specs, out_specs=out_specs, check_vma=False
    )
```

time: 271 us -> 107 us (0.39)
  the two profiles are of different devices: /device:TPU:6 before, /device:TPU:32 now
where the time goes in v1:
time: 107 us; the launch traced here: 106 us
  starting transfers between devices  55.2 us (52%)
  waiting for transfers between devices  33.4 us (31%)
  matrix products  12 us (11%)
  other arithmetic  4.56 us (4%)
    ppermute x12, starting transfers between devices, send(): return lax.ppermute(array, AXES, plan)  55.2 us
    ppermute x12, waiting for transfers between devices, send(): return lax.ppermute(array, AXES, plan)  33.4 us
    dot_general x6, matrix products, dot(): jnp.dot(weights.astype(jnp.bfloat16), cols, preferred_element_type=jnp.fl...  4.66 us
    dot_general x6, matrix products, dot_t(): jnp.einsum('rc,re->ce', weights.astype(jnp.bfloat16), rows, preferred_ele...  4.23 us
    dot_general x6, matrix products, scores_of(): jnp.einsum('re,ce->rc', rows, cols, preferred_element_type=jnp.float32)  3.11 us
  transfers between devices with their start and end apart: 12, of which 5 were waited for; matrix products, arithmetic and copies ran while one was open for 12% of the time, Pallas kernels for 0%

profile of v1, /device:TPU:32, one launch (start us, length us, event | category | flops | bytes accessed | tf_op | source)
XLA Modules:
  0.0 106.2 jit_solution(9950993833064407419)
XLA Ops:
  0.6 2.1 %fusion.12 = bf16[384,768]{1,0:T(8,128)(2,1)} fusion(bf16[384,768]{1,0:T(8,128)(2,1)} %param.2), kind=kLoop, calls=%fused_computation.27 | loop fusion | flops 589824 | bytes 1179648 | tf_op jit(solution)/shard_map/convert_element_type | solution.py:73
  2.8 2.3 %collective-permute-start.1 = (bf16[384,768]{1,0:T(8,128)(2,1)}, bf16[384,768]{1,0:T(8,128)(2,1)S(1)}, u32[]{:S(2)}, u32[]{:S(2)}) collective-permute-start(bf16[384,768]{1,0:T(8,128)(2,1)} %fusion.12), channel_id=1, source_target_pairs={{0,28},{1,29},{2,30},{3,31},{4,0},{5,1},{6,2},{7,3},{8,4},{9,5},{1... | collective-permute-start | bytes 1769480 | tf_op jit(solution)/shard_map/ppermute | solution.py:67
  5.1 1.0 fusion.11
  6.1 6.1 %collective-permute-start.2 = (bf16[384,768]{1,0:T(8,128)(2,1)}, bf16[384,768]{1,0:T(8,128)(2,1)S(1)}, u32[]{:S(2)}, u32[]{:S(2)}) collective-permute-start(bf16[384,768]{1,0:T(8,128)(2,1)} %fusion.11), channel_id=1, source_target_pairs={{0,1},{1,0},{2,3},{3,2},{4,5},{5,4},{6,7},{7,6},{8,9},{9,8},{10,11... | collective-permute-start | bytes 1769480 | tf_op jit(solution)/shard_map/ppermute | solution.py:67
  12.2 7.2 %collective-permute-start.3 = (bf16[384,768]{1,0:T(8,128)(2,1)}, bf16[384,768]{1,0:T(8,128)(2,1)S(1)}, u32[]{:S(2)}, u32[]{:S(2)}) collective-permute-start(bf16[384,768]{1,0:T(8,128)(2,1)} %fusion.12), channel_id=1, source_target_pairs={{0,31},{1,30},{2,1},{3,0},{4,3},{5,2},{6,5},{7,4},{8,7},{9,6},{10,... | collective-permute-start | bytes 1769480 | tf_op jit(solution)/shard_map/ppermute | solution.py:67
  19.4 1.9 %collective-permute-start = (bf16[384,768]{1,0:T(8,128)(2,1)}, bf16[384,768]{1,0:T(8,128)(2,1)S(1)}, u32[]{:S(2)}, u32[]{:S(2)}) collective-permute-start(bf16[384,768]{1,0:T(8,128)(2,1)} %fusion.11), channel_id=1, source_target_pairs={{0,32},{1,33},{2,34},{3,35},{4,36},{5,37},{6,38},{7,39},{8,40},{9,... | collective-permute-start | bytes 1769480 | tf_op jit(solution)/shard_map/ppermute | solution.py:67
  22.0 13.3 %collective-permute-done.2 = bf16[384,768]{1,0:T(8,128)(2,1)S(1)} collective-permute-done((bf16[384,768]{1,0:T(8,128)(2,1)}, bf16[384,768]{1,0:T(8,128)(2,1)S(1)}, u32[]{:S(2)}, u32[]{:S(2)}) %collective-permute-start.2) | collective-permute-done | bytes 589856 | tf_op jit(solution)/shard_map/ppermute | solution.py:67
  36.6 3.4 %collective-permute-start.5 = (f32[2,384]{1,0:T(2,128)S(1)}, f32[2,384]{1,0:T(2,128)S(1)}, u32[]{:S(2)}, u32[]{:S(2)}) collective-permute-start(f32[2,384]{1,0:T(2,128)S(1)} %pad_maximum_fusion.1), channel_id=1, source_target_pairs={{28,0},{29,1},{30,2},{31,3},{0,4},{1,5},{2,6},{3,7},{4,8},{5,9},{6... | collective-permute-start | bytes 9224 | tf_op jit(solution)/shard_map/ppermute | solution.py:67
  40.0 1.6 %collective-permute-done.3 = bf16[384,768]{1,0:T(8,128)(2,1)S(1)} collective-permute-done((bf16[384,768]{1,0:T(8,128)(2,1)}, bf16[384,768]{1,0:T(8,128)(2,1)S(1)}, u32[]{:S(2)}, u32[]{:S(2)}) %collective-permute-start.3) | collective-permute-done | bytes 589856 | tf_op jit(solution)/shard_map/ppermute | solution.py:67
  42.9 12.1 %collective-permute-start.4 = (f32[2,384]{1,0:T(2,128)S(1)}, f32[2,384]{1,0:T(2,128)S(1)}, u32[]{:S(2)}, u32[]{:S(2)}) collective-permute-start(f32[2,384]{1,0:T(2,128)S(1)} %pad_maximum_fusion), channel_id=1, source_target_pairs={{31,0},{30,1},{1,2},{0,3},{3,4},{2,5},{5,6},{4,7},{7,8},{6,9},{9,1... | collective-permute-start | bytes 9224 | tf_op jit(solution)/shard_map/ppermute | solution.py:67
  55.6 0.6 add_convert_fusion
  56.2 2.6 %collective-permute-start.7 = (bf16[384,768]{1,0:T(8,128)(2,1)S(1)}, bf16[384,768]{1,0:T(8,128)(2,1)S(1)}, u32[]{:S(2)}, u32[]{:S(2)}) collective-permute-start(bf16[384,768]{1,0:T(8,128)(2,1)S(1)} %add_convert_fusion), channel_id=1, source_target_pairs={{28,0},{29,1},{30,2},{31,3},{0,4},{1,5},{2,6},{3,7},{4,8},{5,9},{6... | collective-permute-start | bytes 1769480 | tf_op jit(solution)/shard_map/ppermute | solution.py:67
  59.8 1.9 %collective-permute-start.6 = (bf16[384,768]{1,0:T(8,128)(2,1)S(1)}, bf16[384,768]{1,0:T(8,128)(2,1)S(1)}, u32[]{:S(2)}, u32[]{:S(2)}) collective-permute-start(bf16[384,768]{1,0:T(8,128)(2,1)S(1)} %fusion.9), channel_id=1, source_target_pairs={{31,0},{30,1},{1,2},{0,3},{3,4},{2,5},{5,6},{4,7},{7,8},{6,9},{9,1... | collective-permute-start | bytes 1769480 | tf_op jit(solution)/shard_map/ppermute | solution.py:67
  62.5 0.6 fusion.50
  63.1 4.5 %collective-permute-start.8 = (f32[384]{0:T(512)S(1)}, f32[384]{0:T(512)S(1)}, u32[]{:S(2)}, u32[]{:S(2)}) collective-permute-start(f32[384]{0:T(512)S(1)} %get-tuple-element.10), channel_id=1, source_target_pairs={{0,28},{1,29},{2,30},{3,31},{4,0},{5,1},{6,2},{7,3},{8,4},{9,5},{1... | collective-permute-start | bytes 4616 | tf_op jit(solution)/shard_map/ppermute | solution.py:67
  67.6 6.9 %collective-permute-start.9 = (f32[384]{0:T(512)S(1)}, f32[384]{0:T(512)S(1)}, u32[]{:S(2)}, u32[]{:S(2)}) collective-permute-start(f32[384]{0:T(512)S(1)} %get-tuple-element.10), channel_id=1, source_target_pairs={{0,31},{1,30},{2,1},{3,0},{4,3},{5,2},{6,5},{7,4},{8,7},{9,6},{10,... | collective-permute-start | bytes 4616 | tf_op jit(solution)/shard_map/ppermute | solution.py:67
  75.0 0.6 fusion.29
  76.2 4.4 %collective-permute-start.11 = (bf16[384,768]{1,0:T(8,128)(2,1)S(1)}, bf16[384,768]{1,0:T(8,128)(2,1)S(1)}, u32[]{:S(2)}, u32[]{:S(2)}) collective-permute-start(bf16[384,768]{1,0:T(8,128)(2,1)S(1)} %convolution_convert_fusion), channel_id=1, source_target_pairs={{32,0},{33,1},{34,2},{35,3},{36,4},{37,5},{38,6},{39,7},{40,8},{41... | collective-permute-start | bytes 1769480 | tf_op jit(solution)/shard_map/ppermute | solution.py:67
  81.6 1.9 %collective-permute-start.10 = (bf16[384,768]{1,0:T(8,128)(2,1)S(1)}, bf16[384,768]{1,0:T(8,128)(2,1)S(1)}, u32[]{:S(2)}, u32[]{:S(2)}) collective-permute-start(bf16[384,768]{1,0:T(8,128)(2,1)S(1)} %fusion.10), channel_id=1, source_target_pairs={{0,1},{1,0},{2,3},{3,2},{4,5},{5,4},{6,7},{7,6},{8,9},{9,8},{10,11... | collective-permute-start | bytes 1769480 | tf_op jit(solution)/shard_map/ppermute | solution.py:67
  84.0 2.1 %collective-permute-done.6 = bf16[384,768]{1,0:T(8,128)(2,1)S(1)} collective-permute-done((bf16[384,768]{1,0:T(8,128)(2,1)S(1)}, bf16[384,768]{1,0:T(8,128)(2,1)S(1)}, u32[]{:S(2)}, u32[]{:S(2)}) %collective-permute-start.6) | collective-permute-done | bytes 589856 | tf_op jit(solution)/shard_map/ppermute | solution.py:67
  86.1 1.9 %fusion.8 = f32[384,768]{1,0:T(8,128)} fusion(f32[384,768]{1,0:T(8,128)S(1)} %fusion.29, bf16[384,768]{1,0:T(8,128)(2,1)S(1)} %collective-permute-done, bf16[384,768]{1,0:T(8,128)(2,1)S(1)} %collective-permute-done.7, bf16[384,768]{1,0:T(8,128)(2,1)S(1)} %collective-permute-done.6, f32[384,768]{1,0:T(8,128)S(1)} %fusion.15, ...), kind=kOutput, calls=%fused_computation.13 | convolution fusion | flops 230916096 | bytes 6494208 | tf_op jit(solution)/shard_map/dot_general | solution.py:33
  88.1 7.1 %collective-permute-done.11 = bf16[384,768]{1,0:T(8,128)(2,1)S(1)} collective-permute-done((bf16[384,768]{1,0:T(8,128)(2,1)S(1)}, bf16[384,768]{1,0:T(8,128)(2,1)S(1)}, u32[]{:S(2)}, u32[]{:S(2)}) %collective-permute-start.11) | collective-permute-done | bytes 589856 | tf_op jit(solution)/shard_map/ppermute | solution.py:67
  95.1 9.4 %collective-permute-done.10 = bf16[384,768]{1,0:T(8,128)(2,1)S(1)} collective-permute-done((bf16[384,768]{1,0:T(8,128)(2,1)S(1)}, bf16[384,768]{1,0:T(8,128)(2,1)S(1)}, u32[]{:S(2)}, u32[]{:S(2)}) %collective-permute-start.10) | collective-permute-done | bytes 589856 | tf_op jit(solution)/shard_map/ppermute | solution.py:67
  104.5 1.7 %fusion.4 = f32[384,768]{1,0:T(8,128)} fusion(f32[384,768]{1,0:T(8,128)S(1)} %convolution_add_fusion.2, bf16[384,768]{1,0:T(8,128)(2,1)S(1)} %collective-permute-done.3, bf16[384,768]{1,0:T(8,128)(2,1)S(1)} %collective-permute-done.11, bf16[384,768]{1,0:T(8,128)(2,1)S(1)} %collective-permute-done.10, bf16[384,768]{1,0:T(8,128)(2,1)S(1)} %copy-done.1, ...), kind=kOutput, calls=%fused_computation.9 | convolution fusion | flops 229736448 | bytes 5309952 | tf_op jit(solution)/shard_map/rc,re->ce/dot_general | solution.py:39
  (41 shorter events, 8.2 us)
Async XLA Ops:
  0.6 20.7 %copy-start = (bf16[384,768]{1,0:T(8,128)(2,1)S(1)}, bf16[384,768]{1,0:T(8,128)(2,1)}, u32[]{:S(2)}) copy-start(bf16[384,768]{1,0:T(8,128)(2,1)} %param.2) | copy-start | bytes 1769476
  0.6 4.5 %copy-start.1 = (bf16[384,768]{1,0:T(8,128)(2,1)S(1)}, bf16[384,768]{1,0:T(8,128)(2,1)}, u32[]{:S(2)}) copy-start(bf16[384,768]{1,0:T(8,128)(2,1)} %param.3) | copy-start | bytes 1769476
  2.8 19.2 %collective-permute-start.1 = (bf16[384,768]{1,0:T(8,128)(2,1)}, bf16[384,768]{1,0:T(8,128)(2,1)S(1)}, u32[]{:S(2)}, u32[]{:S(2)}) collective-permute-start(bf16[384,768]{1,0:T(8,128)(2,1)} %fusion.12), channel_id=1, source_target_pairs={{0,28},{1,29},{2,30},{3,31},{4,0},{5,1},{6,2},{7,3},{8,4},{9,5},{1... | collective-permute-start | bytes 1769480 | tf_op jit(solution)/shard_map/ppermute | solution.py:67
  6.1 29.2 %collective-permute-start.2 = (bf16[384,768]{1,0:T(8,128)(2,1)}, bf16[384,768]{1,0:T(8,128)(2,1)S(1)}, u32[]{:S(2)}, u32[]{:S(2)}) collective-permute-start(bf16[384,768]{1,0:T(8,128)(2,1)} %fusion.11), channel_id=1, source_target_pairs={{0,1},{1,0},{2,3},{3,2},{4,5},{5,4},{6,7},{7,6},{8,9},{9,8},{10,11... | collective-permute-start | bytes 1769480 | tf_op jit(solution)/shard_map/ppermute | solution.py:67
  12.2 29.4 %collective-permute-start.3 = (bf16[384,768]{1,0:T(8,128)(2,1)}, bf16[384,768]{1,0:T(8,128)(2,1)S(1)}, u32[]{:S(2)}, u32[]{:S(2)}) collective-permute-start(bf16[384,768]{1,0:T(8,128)(2,1)} %fusion.12), channel_id=1, source_target_pairs={{0,31},{1,30},{2,1},{3,0},{4,3},{5,2},{6,5},{7,4},{8,7},{9,6},{10,... | collective-permute-start | bytes 1769480 | tf_op jit(solution)/shard_map/ppermute | solution.py:67
  19.4 42.4 %collective-permute-start = (bf16[384,768]{1,0:T(8,128)(2,1)}, bf16[384,768]{1,0:T(8,128)(2,1)S(1)}, u32[]{:S(2)}, u32[]{:S(2)}) collective-permute-start(bf16[384,768]{1,0:T(8,128)(2,1)} %fusion.11), channel_id=1, source_target_pairs={{0,32},{1,33},{2,34},{3,35},{4,36},{5,37},{6,38},{7,39},{8,40},{9,... | collective-permute-start | bytes 1769480 | tf_op jit(solution)/shard_map/ppermute | solution.py:67
  36.6 25.8 %collective-permute-start.5 = (f32[2,384]{1,0:T(2,128)S(1)}, f32[2,384]{1,0:T(2,128)S(1)}, u32[]{:S(2)}, u32[]{:S(2)}) collective-permute-start(f32[2,384]{1,0:T(2,128)S(1)} %pad_maximum_fusion.1), channel_id=1, source_target_pairs={{28,0},{29,1},{30,2},{31,3},{0,4},{1,5},{2,6},{3,7},{4,8},{5,9},{6... | collective-permute-start | bytes 9224 | tf_op jit(solution)/shard_map/ppermute | solution.py:67
  42.9 19.5 %collective-permute-start.4 = (f32[2,384]{1,0:T(2,128)S(1)}, f32[2,384]{1,0:T(2,128)S(1)}, u32[]{:S(2)}, u32[]{:S(2)}) collective-permute-start(f32[2,384]{1,0:T(2,128)S(1)} %pad_maximum_fusion), channel_id=1, source_target_pairs={{31,0},{30,1},{1,2},{0,3},{3,4},{2,5},{5,6},{4,7},{7,8},{6,9},{9,1... | collective-permute-start | bytes 9224 | tf_op jit(solution)/shard_map/ppermute | solution.py:67
  56.2 27.9 %collective-permute-start.7 = (bf16[384,768]{1,0:T(8,128)(2,1)S(1)}, bf16[384,768]{1,0:T(8,128)(2,1)S(1)}, u32[]{:S(2)}, u32[]{:S(2)}) collective-permute-start(bf16[384,768]{1,0:T(8,128)(2,1)S(1)} %add_convert_fusion), channel_id=1, source_target_pairs={{28,0},{29,1},{30,2},{31,3},{0,4},{1,5},{2,6},{3,7},{4,8},{5,9},{6... | collective-permute-start | bytes 1769480 | tf_op jit(solution)/shard_map/ppermute | solution.py:67
  59.8 26.3 %collective-permute-start.6 = (bf16[384,768]{1,0:T(8,128)(2,1)S(1)}, bf16[384,768]{1,0:T(8,128)(2,1)S(1)}, u32[]{:S(2)}, u32[]{:S(2)}) collective-permute-start(bf16[384,768]{1,0:T(8,128)(2,1)S(1)} %fusion.9), channel_id=1, source_target_pairs={{31,0},{30,1},{1,2},{0,3},{3,4},{2,5},{5,6},{4,7},{7,8},{6,9},{9,1... | collective-permute-start | bytes 1769480 | tf_op jit(solution)/shard_map/ppermute | solution.py:67
  63.1 17.5 %collective-permute-start.8 = (f32[384]{0:T(512)S(1)}, f32[384]{0:T(512)S(1)}, u32[]{:S(2)}, u32[]{:S(2)}) collective-permute-start(f32[384]{0:T(512)S(1)} %get-tuple-element.10), channel_id=1, source_target_pairs={{0,28},{1,29},{2,30},{3,31},{4,0},{5,1},{6,2},{7,3},{8,4},{9,5},{1... | collective-permute-start | bytes 4616 | tf_op jit(solution)/shard_map/ppermute | solution.py:67
  67.6 13.6 %collective-permute-start.9 = (f32[384]{0:T(512)S(1)}, f32[384]{0:T(512)S(1)}, u32[]{:S(2)}, u32[]{:S(2)}) collective-permute-start(f32[384]{0:T(512)S(1)} %get-tuple-element.10), channel_id=1, source_target_pairs={{0,31},{1,30},{2,1},{3,0},{4,3},{5,2},{6,5},{7,4},{8,7},{9,6},{10,... | collective-permute-start | bytes 4616 | tf_op jit(solution)/shard_map/ppermute | solution.py:67
  76.2 19.0 %collective-permute-start.11 = (bf16[384,768]{1,0:T(8,128)(2,1)S(1)}, bf16[384,768]{1,0:T(8,128)(2,1)S(1)}, u32[]{:S(2)}, u32[]{:S(2)}) collective-permute-start(bf16[384,768]{1,0:T(8,128)(2,1)S(1)} %convolution_convert_fusion), channel_id=1, source_target_pairs={{32,0},{33,1},{34,2},{35,3},{36,4},{37,5},{38,6},{39,7},{40,8},{41... | collective-permute-start | bytes 1769480 | tf_op jit(solution)/shard_map/ppermute | solution.py:67
  81.6 22.9 %collective-permute-start.10 = (bf16[384,768]{1,0:T(8,128)(2,1)S(1)}, bf16[384,768]{1,0:T(8,128)(2,1)S(1)}, u32[]{:S(2)}, u32[]{:S(2)}) collective-permute-start(bf16[384,768]{1,0:T(8,128)(2,1)S(1)} %fusion.10), channel_id=1, source_target_pairs={{0,1},{1,0},{2,3},{3,2},{4,5},{5,4},{6,7},{7,6},{8,9},{9,8},{10,11... | collective-permute-start | bytes 1769480 | tf_op jit(solution)/shard_map/ppermute | solution.py:67

commit v2 on v1

v2 whole, which is shorter than its diff:
```python
import jax
import jax.numpy as jnp
from jax import lax
from jax.experimental import pallas as pl
from jax.experimental.pallas import tpu as pltpu
from jax.sharding import PartitionSpec as P

logit_scale = 0.32
AXES = ("group", "blk")
LOW = -1e30
TAIL = 16
LIMIT = 6 << 20
F32 = jnp.float32
BF16 = jnp.bfloat16


def scores_t(text, image):
    return logit_scale * lax.dot_general(
        text, image, (((1,), (1,)), ((), ())), preferred_element_type=F32
    )


def image_term(weights_t, text):
    return lax.dot_general(
        weights_t.astype(BF16), text, (((0,), (0,)), ((), ())), preferred_element_type=F32
    )


def text_term(weights_t, image):
    return jnp.dot(weights_t.astype(BF16), image, preferred_element_type=F32)


def soft_of(pre):
    return jnp.tanh(pre[...].astype(F32))


def peak_of(*blocks):
    peak = jnp.max(blocks[0], axis=0, keepdims=True)
    for block in blocks[1:]:
        peak = jnp.maximum(peak, jnp.max(block, axis=0, keepdims=True))
    return peak


def total_of(weights):
    return jnp.sum(weights, axis=0, keepdims=True)


def merge(first, second):
    peak = jnp.maximum(first[0], second[0])
    total = first[1] * jnp.exp(first[0] - peak) + second[1] * jnp.exp(second[0] - peak)
    return peak, total


def close(first, second, third):
    peak, total = merge(merge(first, second), third)
    return peak + jnp.log(total)


def column(row):
    wide = jnp.broadcast_to(row, (128, row.shape[1]))
    return jnp.transpose(wide)[:, :1]


def pair(ref, at=0):
    return ref[at : at + 1, :], ref[at + 1 : at + 2, :]


def pack(out, part, stats):
    rows, width = part.shape
    out[:rows, :] = part.astype(BF16)
    place = lax.broadcasted_iota(jnp.int32, (TAIL, rows), 0)
    tail = jnp.zeros((TAIL, rows), F32)
    spot = 0
    for stat in stats:
        for _ in range(3):
            piece = stat.astype(BF16).astype(F32)
            tail = jnp.where(place == spot, piece, tail)
            stat = stat - piece
            spot += 1
    out[rows:, :rows] = tail.astype(BF16)
    out[rows:, rows:] = jnp.zeros((TAIL, width - rows), BF16)


def unpack(tail, spot, rows):
    tail = tail[:, :rows].astype(F32)

    def row(at):
        return tail[at : at + 1] + tail[at + 1 : at + 2] + tail[at + 2 : at + 3]

    return row(6 * spot), row(6 * spot + 3)


def hop_kernel(text, pre_hop, image_h, s_h, packed):
    image = soft_of(pre_hop).astype(BF16)
    image_h[...] = image
    scores = scores_t(text[...], image)
    s_h[...] = scores
    peak = peak_of(scores)
    weights = jnp.exp(scores - peak)
    pack(packed, image_term(weights, text[...]), (peak, total_of(weights)))


def soft_kernel(pre_img, pre_txt, image, text):
    image[...] = soft_of(pre_img).astype(BF16)
    text[...] = soft_of(pre_txt).astype(BF16)


def early_kernel(
    even, image, text, pre_p, pre_v,
    text_p, image_v, s_own, s_v, s_y, stat_v, stat_o, packed,
):
    is_even = even[0] == 1
    img = image[...]
    txt = text[...]
    other = soft_of(pre_p).astype(BF16)
    img_v = soft_of(pre_v).astype(BF16)
    text_p[...] = other
    image_v[...] = img_v
    sv = scores_t(txt, img_v)
    s_v[...] = sv
    sy = scores_t(other, jnp.where(is_even, img_v, img))
    s_y[...] = sy
    sy_v = jnp.where(is_even, sy, LOW)
    peak = peak_of(sv, sy_v)
    first = jnp.exp(sv - peak)
    second = jnp.exp(sy_v - peak)
    total = total_of(first) + total_of(second)
    stat_v[0:1, :] = peak
    stat_v[1:2, :] = total
    pack(packed, image_term(first, txt) + image_term(second, other), (peak, total))
    so = scores_t(txt, img)
    s_own[...] = so
    sy_o = jnp.where(is_even, LOW, sy)
    peak = peak_of(so, sy_o)
    stat_o[0:1, :] = peak
    stat_o[1:2, :] = total_of(jnp.exp(so - peak)) + total_of(jnp.exp(sy_o - peak))


def home_kernel(stat_o, stat_x, home_h, stat_i, stat_c):
    rows = stat_o.shape[1]
    peak, total = merge(pair(stat_o), unpack(home_h[rows:, :], 0, rows))
    stat_i[0:1, :] = peak
    stat_i[1:2, :] = total
    stat_c[0:1, :] = peak
    stat_c[1:2, :] = total
    stat_c[2:4, :] = stat_x[...]


def late_kernel(image_x, text, text_p, stat_v, s_xt, s_xp, stat_x, packed):
    img = image_x[...]
    first = scores_t(text[...], img)
    second = scores_t(text_p[...], img)
    s_xt[...] = first
    s_xp[...] = second
    peak = peak_of(first, second)
    first = jnp.exp(first - peak)
    second = jnp.exp(second - peak)
    total = total_of(first) + total_of(second)
    part = image_term(first, text[...]) + image_term(second, text_p[...])
    pack(packed, part, (peak, total) + pair(stat_v))
    stat_x[0:1, :] = peak
    stat_x[1:2, :] = total


def lse_kernel(
    even, stat_c, stat_v, from_i, from_u, home_x, home_v,
    s_xp, s_y, image_x, image_v, image, term_p, lse_i, lse_xv,
):
    is_even = even[0] == 1
    rows = stat_c.shape[1]
    tail_c, tail_v = home_x[rows:, :], home_v[rows:, :]
    own = close(pair(stat_c), unpack(tail_c, 0, rows), unpack(tail_v, 0, rows))
    of_x = close(pair(from_u), pair(stat_c, 2), unpack(tail_c, 1, rows))
    of_v = close(pair(from_i), pair(from_u, 2), pair(stat_v))
    lse_i[...] = own
    lse_xv[0:1, :] = of_x
    lse_xv[1:2, :] = of_v
    of_y = jnp.where(is_even, of_v, own)
    img_y = jnp.where(is_even, image_v[...], image[...])
    term = text_term(jnp.exp(s_xp[...] - of_x), image_x[...])
    term_p[...] = (term + text_term(jnp.exp(s_y[...] - of_y), img_y)).astype(BF16)


def image_kernel(
    even, pre_img, lse_i, s_own, s_y, text, text_p, home_x, home_v, home_h,
    grad_img, row_loss,
):
    is_even = even[0] == 1
    rows = text.shape[0]
    lse = lse_i[...]
    so = s_own[...]
    eye = lax.broadcasted_iota(jnp.int32, so.shape, 0) == lax.broadcasted_iota(
        jnp.int32, so.shape, 1
    )
    row_loss[...] = lse - jnp.sum(jnp.where(eye, so, 0.0), axis=0, keepdims=True)
    grad = image_term(jnp.exp(so - lse) - eye.astype(F32), text[...])
    sy = jnp.where(is_even, LOW, s_y[...])
    grad += image_term(jnp.exp(sy - lse), text_p[...])
    for home in (home_x, home_v, home_h):
        peak, _ = unpack(home[rows:, :], 0, rows)
        grad += home[:rows, :].astype(F32) * column(jnp.exp(peak - lse))
    soft = soft_of(pre_img)
    grad_img[...] = logit_scale * grad * (1.0 - soft * soft)


def text_kernel(
    pre_txt, lse_i, lse_xv, s_own, s_v, s_xt, image, image_v, image_x, text_sum, slope, lse_out
):
    so = s_own[...]
    eye = lax.broadcasted_iota(jnp.int32, so.shape, 0) == lax.broadcasted_iota(
        jnp.int32, so.shape, 1
    )
    term = text_term(jnp.exp(so - lse_i[...]) - eye.astype(F32), image[...])
    term += text_term(jnp.exp(s_xt[...] - lse_xv[0:1, :]), image_x[...])
    term += text_term(jnp.exp(s_v[...] - lse_xv[1:2, :]), image_v[...])
    text_sum[...] = term
    lse_out[...] = lse_i[...]
    soft = soft_of(pre_txt)
    slope[...] = logit_scale * (1.0 - soft * soft)


def more_kernel(text_sum, lse_h, s_h, image_h, text_all):
    text_all[...] = text_sum[...] + text_term(jnp.exp(s_h[...] - lse_h[...]), image_h[...])


def last_kernel(text_all, slope, got_p, grad_txt):
    grad_txt[...] = (text_all[...] + got_p[...].astype(F32)) * slope[...]


def together(*arrays):
    return lax.optimization_barrier(arrays)


def solution(mesh):
    groups, blks = mesh.shape["group"], mesh.shape["blk"]

    def even_at(g, b):
        return (g + b) % 2 == 0

    def pairs(move):
        out = []
        for g in range(groups):
            for b in range(blks):
                to_g, to_b = move(g, b)
                out.append((g * blks + b, (to_g % groups) * blks + to_b % blks))
        return out

    swap = pairs(lambda g, b: (g, b + 1 if even_at(g, b) else b - 1))
    cross = pairs(lambda g, b: (g, b - 1 if even_at(g, b) else b - 3))
    uncross = [(t, s) for s, t in cross]
    back = pairs(lambda g, b: (g, b - 4))
    forth = [(t, s) for s, t in back]
    unhop = pairs(lambda g, b: (g - 1, b))
    hop = [(t, s) for s, t in unhop]

    def send(array, plan):
        return lax.ppermute(array, AXES, plan)

    def run(kernel, outs, *args, matmuls=0, name=None):
        vmem = pl.BlockSpec(memory_space=pltpu.VMEM)
        smem = pl.BlockSpec(memory_space=pltpu.SMEM)
        return pl.pallas_call(
            kernel,
            out_shape=outs,
            in_specs=[smem if v.dtype == jnp.int32 else vmem for v in args],
            out_specs=[vmem] * len(outs),
            compiler_params=pltpu.CompilerParams(vmem_limit_bytes=LIMIT),
            cost_estimate=pl.CostEstimate(
                flops=matmuls * 2 * 384 * 384 * 768, bytes_accessed=0, transcendentals=0
            ),
            name=name,
        )(*args)

    def per_device(pre_img, pre_txt):
        rows, width = pre_img.shape
        block = jax.ShapeDtypeStruct((rows, width), BF16)
        packed = jax.ShapeDtypeStruct((rows + TAIL, width), BF16)
        wide = jax.ShapeDtypeStruct((rows, width), F32)
        square = jax.ShapeDtypeStruct((rows, rows), F32)

        def stat(count):
            return jax.ShapeDtypeStruct((count, rows), F32)

        even = (lax.axis_index("group") + lax.axis_index("blk")) % 2 == 0
        even = even.astype(jnp.int32).reshape(1)

        pre_h = send(pre_img, unhop)
        pre_v = send(pre_img, back)
        pre_p = send(pre_txt, swap)
        image, text = run(soft_kernel, (block, block), pre_img, pre_txt, name="soft")
        pre_p, img_x = together(pre_p, image)
        image_x = send(img_x, cross)

        text_p, image_v, s_own, s_v, s_y, stat_v, stat_o, part_v = run(
            early_kernel,
            (block, block, square, square, square, stat(2), stat(2), packed),
            even, image, text, pre_p, pre_v, matmuls=5, name="early",
        )
        home_v = send(part_v, forth)
        text_p, pre_h = together(text_p, pre_h)
        image_h, s_h, part_h = run(
            hop_kernel, (block, square, packed), text, pre_h, matmuls=2, name="hop"
        )
        home_h = send(part_h, hop)
        s_xt, s_xp, stat_x, part_x = run(
            late_kernel,
            (square, square, stat(2), packed),
            image_x, text, text_p, stat_v, matmuls=4, name="late",
        )
        home_x = send(part_x, uncross)
        stat_i, stat_c = run(
            home_kernel, (stat(2), stat(4)), stat_o, stat_x, home_h, name="home"
        )
        from_i = send(stat_i, back)
        from_u = send(stat_c, cross)
        term_p, lse_i, lse_xv = run(
            lse_kernel,
            (block, stat(1), stat(2)),
            even, stat_c, stat_v, from_i, from_u, home_x, home_v,
            s_xp, s_y, image_x, image_v, image, matmuls=2, name="lse",
        )
        got_p = send(term_p, swap)
        grad_img, row_loss = run(
            image_kernel,
            (wide, stat(1)),
            even, pre_img, lse_i, s_own, s_y, text, text_p, home_x, home_v, home_h,
            matmuls=2, name="image",
        )
        text_sum, slope, lse_out = run(
            text_kernel,
            (wide, wide, stat(1)),
            pre_txt, lse_i, lse_xv, s_own, s_v, s_xt, image, image_v, image_x,
            matmuls=3, name="text",
        )
        lse_h = send(lse_out, unhop)
        (text_all,) = run(
            more_kernel, (wide,), text_sum, lse_h, s_h, image_h, matmuls=1, name="more"
        )
        (grad_txt,) = run(last_kernel, (wide,), text_all, slope, got_p, name="last")
        return grad_img, grad_txt, row_loss.reshape(rows)

    in_specs = (P(AXES, None), P(AXES, None))
    out_specs = (P(AXES, None), P(AXES, None), P(AXES))
    return jax.shard_map(
        per_device, mesh=mesh, in_specs=in_specs, out_specs=out_specs, check_vma=False
    )
```

time: 107 us -> 97 us (0.907)
  the two profiles are of different devices: /device:TPU:32 before, /device:TPU:6 now
where the time goes in v2:
time: 97 us; the launch traced here: 96.5 us
  starting transfers between devices  53.6 us (55%)
  waiting for transfers between devices  25.6 us (26%)
  Pallas kernels  13.6 us (14%)
  local copies, waits for them, and re-layouts  2.16 us (2%)
    ppermute x11, starting transfers between devices, send(): return lax.ppermute(array, AXES, plan)  53.6 us
    ppermute x11, waiting for transfers between devices, send(): return lax.ppermute(array, AXES, plan)  25.6 us
    pallas_call x10, Pallas kernels, run(): pl.pallas_call(kernel, out_shape=outs, in_specs=[smem if v.dtype == jnp.i...  13.6 us
    unnamed x20, local copies, waits for them, and re-layouts  2.16 us
  transfers between devices with their start and end apart: 11, of which 5 were waited for; matrix products, arithmetic and copies ran while one was open for 1% of the time, Pallas kernels for 10%

profile of v2, /device:TPU:6, one launch (start us, length us, event | category | flops | bytes accessed | tf_op | source)
XLA Modules:
  0.0 96.5 jit_solution(13183770104829044724)
XLA Ops:
  0.6 6.1 %collective-permute-start = (bf16[384,768]{1,0:T(8,128)(2,1)}, bf16[384,768]{1,0:T(8,128)(2,1)S(1)}, u32[]{:S(2)}, u32[]{:S(2)}) collective-permute-start(bf16[384,768]{1,0:T(8,128)(2,1)} %pre_txt.3), channel_id=1, source_target_pairs={{0,1},{1,0},{2,3},{3,2},{4,5},{5,4},{6,7},{7,6},{8,9},{9,8},{10,11... | collective-permute-start | bytes 1769480 | tf_op jit(solution)/shard_map/ppermute | solution.py:257
  6.7 5.4 %collective-permute-start.1 = (bf16[384,768]{1,0:T(8,128)(2,1)}, bf16[384,768]{1,0:T(8,128)(2,1)S(1)}, u32[]{:S(2)}, u32[]{:S(2)}) collective-permute-start(bf16[384,768]{1,0:T(8,128)(2,1)} %pre_img.3), channel_id=1, source_target_pairs={{0,28},{1,29},{2,30},{3,31},{4,0},{5,1},{6,2},{7,3},{8,4},{9,5},{1... | collective-permute-start | bytes 1769480 | tf_op jit(solution)/shard_map/ppermute | solution.py:257
  12.1 7.3 %collective-permute-start.3 = (bf16[384,768]{1,0:T(8,128)(2,1)}, bf16[384,768]{1,0:T(8,128)(2,1)S(1)}, u32[]{:S(2)}, u32[]{:S(2)}) collective-permute-start(bf16[384,768]{1,0:T(8,128)(2,1)} %pre_img.3), channel_id=1, source_target_pairs={{0,480},{1,481},{2,482},{3,483},{4,484},{5,485},{6,486},{7,487},{8... | collective-permute-start | bytes 1769480 | tf_op jit(solution)/shard_map/ppermute | solution.py:257
  19.4 1.1 %copy-done = bf16[384,768]{1,0:T(8,128)(2,1)S(1)} copy-done((bf16[384,768]{1,0:T(8,128)(2,1)S(1)}, bf16[384,768]{1,0:T(8,128)(2,1)}, u32[]{:S(2)}) %copy-start) | copy-done | bytes 589848
  20.4 1.1 %copy-done.2 = bf16[384,768]{1,0:T(8,128)(2,1)S(1)} copy-done((bf16[384,768]{1,0:T(8,128)(2,1)S(1)}, bf16[384,768]{1,0:T(8,128)(2,1)}, u32[]{:S(2)}) %copy-start.2) | copy-done | bytes 589848
  22.6 11.1 %collective-permute-start.2 = (bf16[384,768]{1,0:T(8,128)(2,1)S(1)}, bf16[384,768]{1,0:T(8,128)(2,1)S(1)}, u32[]{:S(2)}, u32[]{:S(2)}) collective-permute-start(bf16[384,768]{1,0:T(8,128)(2,1)S(1)} %get-tuple-element.38.image), channel_id=1, source_target_pairs={{0,31},{1,30},{2,1},{3,0},{4,3},{5,2},{6,5},{7,4},{8,7},{9,6},{10,... | collective-permute-start | bytes 1769480 | tf_op jit(solution)/shard_map/ppermute | solution.py:257
  33.8 2.4 %early.1 = (bf16[384,768]{1,0:T(8,128)(2,1)S(1)}, bf16[384,768]{1,0:T(8,128)(2,1)S(1)}, f32[384,384]{1,0:T(8,128)S(1)}, f32[384,384]{1,0:T(8,128)S(1)}, f32[384,...) custom-call(s32[1]{0:T(128)} %bitcast.even, ...), custom_call_target="tpu_custom_call" | custom-call | flops 1132462080 | tf_op jit(solution)/shard_map/early/pallas_call | solution.py:262
  36.2 1.9 %collective-permute-start.8 = (bf16[400,768]{1,0:T(8,128)(2,1)S(1)}, bf16[400,768]{1,0:T(8,128)(2,1)S(1)}, u32[]{:S(2)}, u32[]{:S(2)}) collective-permute-start(bf16[400,768]{1,0:T(8,128)(2,1)S(1)} %get-tuple-element.48), channel_id=1, source_target_pairs={{28,0},{29,1},{30,2},{31,3},{0,4},{1,5},{2,6},{3,7},{4,8},{5,9},{6... | collective-permute-start | bytes 1843208 | tf_op jit(solution)/shard_map/ppermute | solution.py:257
  38.1 1.1 %hop.1 = (bf16[384,768]{1,0:T(8,128)(2,1)S(1)}, f32[384,384]{1,0:T(8,128)S(1)}, bf16[400,768]{1,0:T(8,128)(2,1)S(1)}) custom-call(bf16[384,768]{1,0:T(8,128)(2,1)S(1)} %get-tuple-element.35.text, bf16[384,768]{1,0:T(8,128)(2,1)S(1)} %collective-permute-done.3.pre_hop), custom_call_target="tpu_custom_call" | custom-call | flops 452984832 | tf_op jit(solution)/shard_map/hop/pallas_call | solution.py:262
  39.2 1.9 %collective-permute-start.4 = (bf16[400,768]{1,0:T(8,128)(2,1)S(1)}, bf16[400,768]{1,0:T(8,128)(2,1)S(1)}, u32[]{:S(2)}, u32[]{:S(2)}) collective-permute-start(bf16[400,768]{1,0:T(8,128)(2,1)S(1)} %get-tuple-element.44), channel_id=1, source_target_pairs={{480,0},{481,1},{482,2},{483,3},{484,4},{485,5},{486,6},{487,7},{4... | collective-permute-start | bytes 1843208 | tf_op jit(solution)/shard_map/ppermute | solution.py:257
  41.1 4.1 %collective-permute-done.2.image_x = bf16[384,768]{1,0:T(8,128)(2,1)S(1)} collective-permute-done((bf16[384,768]{1,0:T(8,128)(2,1)S(1)}, bf16[384,768]{1,0:T(8,128)(2,1)S(1)}, u32[]{:S(2)}, u32[]{:S(2)}) %collective-permute-start.2) | collective-permute-done | bytes 589856 | tf_op jit(solution)/shard_map/ppermute | solution.py:257
  45.2 1.9 %late.1 = (f32[384,384]{1,0:T(8,128)S(1)}, f32[384,384]{1,0:T(8,128)S(1)}, f32[2,384]{1,0:T(2,128)S(1)}, bf16[400,768]{1,0:T(8,128)(2,1)S(1)}) custom-call(bf16[384,768]{1,0:T(8,128)(2,1)S(1)} %collective-permute-done.2.image_x, bf16[384,768]{1,0:T(8,128)(2,1)S(1)} %get-tuple-element.35.text, bf16[384,768]{1,0:T(8,128)(2,1)S(1)} %get-tuple-element.40.text_p, ...), custom_call_target="tpu_custom_call" | custom-call | flops 905969664 | tf_op jit(solution)/shard_map/late/pallas_call | solution.py:262
  47.1 6.0 %collective-permute-start.7 = (bf16[400,768]{1,0:T(8,128)(2,1)S(1)}, bf16[400,768]{1,0:T(8,128)(2,1)S(1)}, u32[]{:S(2)}, u32[]{:S(2)}) collective-permute-start(bf16[400,768]{1,0:T(8,128)(2,1)S(1)} %get-tuple-element.47), channel_id=1, source_target_pairs={{31,0},{30,1},{1,2},{0,3},{3,4},{2,5},{5,6},{4,7},{7,8},{6,9},{9,1... | collective-permute-start | bytes 1843208 | tf_op jit(solution)/shard_map/ppermute | solution.py:257
  53.1 6.1 %collective-permute-start.6 = (f32[4,384]{1,0:T(4,128)S(1)}, f32[4,384]{1,0:T(4,128)S(1)}, u32[]{:S(2)}, u32[]{:S(2)}) collective-permute-start(f32[4,384]{1,0:T(4,128)S(1)} %get-tuple-element.45.stat_c), channel_id=1, source_target_pairs={{0,31},{1,30},{2,1},{3,0},{4,3},{5,2},{6,5},{7,4},{8,7},{9,6},{10,... | collective-permute-start | bytes 18440 | tf_op jit(solution)/shard_map/ppermute | solution.py:257
  59.2 2.5 %collective-permute-start.5 = (f32[2,384]{1,0:T(2,128)S(1)}, f32[2,384]{1,0:T(2,128)S(1)}, u32[]{:S(2)}, u32[]{:S(2)}) collective-permute-start(f32[2,384]{1,0:T(2,128)S(1)} %get-tuple-element.46), channel_id=1, source_target_pairs={{0,28},{1,29},{2,30},{3,31},{4,0},{5,1},{6,2},{7,3},{8,4},{9,5},{1... | collective-permute-start | bytes 9224 | tf_op jit(solution)/shard_map/ppermute | solution.py:257
  61.7 3.0 %collective-permute-done.5.from_i = f32[2,384]{1,0:T(2,128)S(1)} collective-permute-done((f32[2,384]{1,0:T(2,128)S(1)}, f32[2,384]{1,0:T(2,128)S(1)}, u32[]{:S(2)}, u32[]{:S(2)}) %collective-permute-start.5) | collective-permute-done | bytes 3104 | tf_op jit(solution)/shard_map/ppermute | solution.py:257
  64.7 8.2 %collective-permute-done.7.home_x = bf16[400,768]{1,0:T(8,128)(2,1)S(1)} collective-permute-done((bf16[400,768]{1,0:T(8,128)(2,1)S(1)}, bf16[400,768]{1,0:T(8,128)(2,1)S(1)}, u32[]{:S(2)}, u32[]{:S(2)}) %collective-permute-start.7) | collective-permute-done | bytes 614432 | tf_op jit(solution)/shard_map/ppermute | solution.py:257
  72.9 1.7 %lse.1 = (bf16[384,768]{1,0:T(8,128)(2,1)}, f32[1,384]{1,0:T(1,128)S(1)}, f32[2,384]{1,0:T(2,128)S(1)}) custom-call(s32[1]{0:T(128)} %bitcast.even, f32[4,384]{1,0:T(4,128)S(1)} %get-tuple-element.45.stat_c, f32[2,384]{1,0:T(2,128)S(1)} %get-tuple-element.41.stat_v, f32[2,384]{1,0:T(2,128)S(1)} %collective-permute-done.5.from_i, ...), custom_call_target="tpu_custom_call" | custom-call | flops 452984832 | tf_op jit(solution)/shard_map/lse/pallas_call | solution.py:262
  74.6 1.9 %collective-permute-start.10 = (bf16[384,768]{1,0:T(8,128)(2,1)}, bf16[384,768]{1,0:T(8,128)(2,1)}, u32[]{:S(2)}, u32[]{:S(2)}) collective-permute-start(bf16[384,768]{1,0:T(8,128)(2,1)} %get-tuple-element.63), channel_id=1, source_target_pairs={{0,1},{1,0},{2,3},{3,2},{4,5},{5,4},{6,7},{7,6},{8,9},{9,8},{10,11... | collective-permute-start | bytes 1769480 | tf_op jit(solution)/shard_map/ppermute | solution.py:257
  76.6 1.4 %text.1 = (f32[384,768]{1,0:T(8,128)S(1)}, f32[384,768]{1,0:T(8,128)S(1)}, f32[1,384]{1,0:T(1,128)S(1)}) custom-call(bf16[384,768]{1,0:T(8,128)(2,1)S(1)} %copy-done.1, f32[1,384]{1,0:T(1,128)S(1)} %get-tuple-element.52.lse_i, f32[2,384]{1,0:T(2,128)S(1)} %get-tuple-element.55.lse_xv, f32[384,384]{1,0:T(8,128)S(1)} %get-tuple-element.53.s_own, ...), custom_call_target="tpu_custom_call" | custom-call | flops 679477248 | tf_op jit(solution)/shard_map/text/pallas_call | solution.py:262
  78.0 3.5 %collective-permute-start.9 = (f32[1,384]{1,0:T(1,128)S(1)}, f32[1,384]{1,0:T(1,128)S(1)}, u32[]{:S(2)}, u32[]{:S(2)}) collective-permute-start(f32[1,384]{1,0:T(1,128)S(1)} %get-tuple-element.59), channel_id=1, source_target_pairs={{0,480},{1,481},{2,482},{3,483},{4,484},{5,485},{6,486},{7,487},{8... | collective-permute-start | bytes 4616 | tf_op jit(solution)/shard_map/ppermute | solution.py:257
  81.5 2.2 %image.1 = (f32[384,768]{1,0:T(8,128)}, f32[1,384]{1,0:T(1,128)S(1)}) custom-call(s32[1]{0:T(128)} %bitcast.even, bf16[384,768]{1,0:T(8,128)(2,1)S(1)} %copy-done.3, f32[1,384]{1,0:T(1,128)S(1)} %get-tuple-element.52.lse_i, f32[384,384]{1,0:T(8,128)S(1)} %get-tuple-element.53.s_own, f32[384,384]{1,0:T(8,128)S(1)} %get-tuple-element.50.s_y, ...), custom_call_target="tpu_custom_call" | custom-call | flops 452984832 | tf_op jit(solution)/shard_map/image/pallas_call | solution.py:262
  84.8 9.5 %collective-permute-done.10.got_p = bf16[384,768]{1,0:T(8,128)(2,1)} collective-permute-done((bf16[384,768]{1,0:T(8,128)(2,1)}, bf16[384,768]{1,0:T(8,128)(2,1)}, u32[]{:S(2)}, u32[]{:S(2)}) %collective-permute-start.10) | collective-permute-done | bytes 589856 | tf_op jit(solution)/shard_map/ppermute | solution.py:257
  94.3 2.2 %last.1 = f32[384,768]{1,0:T(8,128)} custom-call(f32[384,768]{1,0:T(8,128)S(1)} %more.1.text_all, f32[384,768]{1,0:T(8,128)S(1)} %get-tuple-element.62.slope, bf16[384,768]{1,0:T(8,128)(2,1)} %collective-permute-done.10.got_p), custom_call_target="tpu_custom_call" | custom-call | tf_op jit(solution)/shard_map/last/pallas_call | solution.py:262
  (29 shorter events, 2.2 us)
Async XLA Ops:
  0.6 22.0 %collective-permute-start = (bf16[384,768]{1,0:T(8,128)(2,1)}, bf16[384,768]{1,0:T(8,128)(2,1)S(1)}, u32[]{:S(2)}, u32[]{:S(2)}) collective-permute-start(bf16[384,768]{1,0:T(8,128)(2,1)} %pre_txt.3), channel_id=1, source_target_pairs={{0,1},{1,0},{2,3},{3,2},{4,5},{5,4},{6,7},{7,6},{8,9},{9,8},{10,11... | collective-permute-start | bytes 1769480 | tf_op jit(solution)/shard_map/ppermute | solution.py:257
  6.7 27.0 %collective-permute-start.1 = (bf16[384,768]{1,0:T(8,128)(2,1)}, bf16[384,768]{1,0:T(8,128)(2,1)S(1)}, u32[]{:S(2)}, u32[]{:S(2)}) collective-permute-start(bf16[384,768]{1,0:T(8,128)(2,1)} %pre_img.3), channel_id=1, source_target_pairs={{0,28},{1,29},{2,30},{3,31},{4,0},{5,1},{6,2},{7,3},{8,4},{9,5},{1... | collective-permute-start | bytes 1769480 | tf_op jit(solution)/shard_map/ppermute | solution.py:257
  12.1 24.0 %collective-permute-start.3 = (bf16[384,768]{1,0:T(8,128)(2,1)}, bf16[384,768]{1,0:T(8,128)(2,1)S(1)}, u32[]{:S(2)}, u32[]{:S(2)}) collective-permute-start(bf16[384,768]{1,0:T(8,128)(2,1)} %pre_img.3), channel_id=1, source_target_pairs={{0,480},{1,481},{2,482},{3,483},{4,484},{5,485},{6,486},{7,487},{8... | collective-permute-start | bytes 1769480 | tf_op jit(solution)/shard_map/ppermute | solution.py:257
  19.4 1.1 %copy-start = (bf16[384,768]{1,0:T(8,128)(2,1)S(1)}, bf16[384,768]{1,0:T(8,128)(2,1)}, u32[]{:S(2)}) copy-start(bf16[384,768]{1,0:T(8,128)(2,1)} %pre_txt.3) | copy-start | bytes 1769476
  20.4 1.1 %copy-start.2 = (bf16[384,768]{1,0:T(8,128)(2,1)S(1)}, bf16[384,768]{1,0:T(8,128)(2,1)}, u32[]{:S(2)}) copy-start(bf16[384,768]{1,0:T(8,128)(2,1)} %pre_img.3) | copy-start | bytes 1769476
  21.8 23.3 %copy-start.4 = (bf16[384,768]{1,0:T(8,128)(2,1)}, bf16[384,768]{1,0:T(8,128)(2,1)S(1)}, u32[]{:S(2)}) copy-start(bf16[384,768]{1,0:T(8,128)(2,1)S(1)} %get-tuple-element.35.text) | copy-start | bytes 1769476
  22.6 22.6 %collective-permute-start.2 = (bf16[384,768]{1,0:T(8,128)(2,1)S(1)}, bf16[384,768]{1,0:T(8,128)(2,1)S(1)}, u32[]{:S(2)}, u32[]{:S(2)}) collective-permute-start(bf16[384,768]{1,0:T(8,128)(2,1)S(1)} %get-tuple-element.38.image), channel_id=1, source_target_pairs={{0,31},{1,30},{2,1},{3,0},{4,3},{5,2},{6,5},{7,4},{8,7},{9,6},{10,... | collective-permute-start | bytes 1769480 | tf_op jit(solution)/shard_map/ppermute | solution.py:257
  36.2 25.5 %collective-permute-start.8 = (bf16[400,768]{1,0:T(8,128)(2,1)S(1)}, bf16[400,768]{1,0:T(8,128)(2,1)S(1)}, u32[]{:S(2)}, u32[]{:S(2)}) collective-permute-start(bf16[400,768]{1,0:T(8,128)(2,1)S(1)} %get-tuple-element.48), channel_id=1, source_target_pairs={{28,0},{29,1},{30,2},{31,3},{0,4},{1,5},{2,6},{3,7},{4,8},{5,9},{6... | collective-permute-start | bytes 1843208 | tf_op jit(solution)/shard_map/ppermute | solution.py:257
  39.2 7.9 %copy-start.6 = (bf16[384,768]{1,0:T(8,128)(2,1)}, bf16[384,768]{1,0:T(8,128)(2,1)S(1)}, u32[]{:S(2)}) copy-start(bf16[384,768]{1,0:T(8,128)(2,1)S(1)} %get-tuple-element.61.image_h) | copy-start | bytes 1769476
  39.2 7.9 %copy-start.8 = (f32[384,384]{1,0:T(8,128)}, f32[384,384]{1,0:T(8,128)S(1)}, u32[]{:S(2)}) copy-start(f32[384,384]{1,0:T(8,128)S(1)} %get-tuple-element.60.s_h) | copy-start | bytes 1769476
  39.2 13.9 %collective-permute-start.4 = (bf16[400,768]{1,0:T(8,128)(2,1)S(1)}, bf16[400,768]{1,0:T(8,128)(2,1)S(1)}, u32[]{:S(2)}, u32[]{:S(2)}) collective-permute-start(bf16[400,768]{1,0:T(8,128)(2,1)S(1)} %get-tuple-element.44), channel_id=1, source_target_pairs={{480,0},{481,1},{482,2},{483,3},{484,4},{485,5},{486,6},{487,7},{4... | collective-permute-start | bytes 1843208 | tf_op jit(solution)/shard_map/ppermute | solution.py:257
  47.1 25.9 %collective-permute-start.7 = (bf16[400,768]{1,0:T(8,128)(2,1)S(1)}, bf16[400,768]{1,0:T(8,128)(2,1)S(1)}, u32[]{:S(2)}, u32[]{:S(2)}) collective-permute-start(bf16[400,768]{1,0:T(8,128)(2,1)S(1)} %get-tuple-element.47), channel_id=1, source_target_pairs={{31,0},{30,1},{1,2},{0,3},{3,4},{2,5},{5,6},{4,7},{7,8},{6,9},{9,1... | collective-permute-start | bytes 1843208 | tf_op jit(solution)/shard_map/ppermute | solution.py:257
  53.1 11.6 %collective-permute-start.6 = (f32[4,384]{1,0:T(4,128)S(1)}, f32[4,384]{1,0:T(4,128)S(1)}, u32[]{:S(2)}, u32[]{:S(2)}) collective-permute-start(f32[4,384]{1,0:T(4,128)S(1)} %get-tuple-element.45.stat_c), channel_id=1, source_target_pairs={{0,31},{1,30},{2,1},{3,0},{4,3},{5,2},{6,5},{7,4},{8,7},{9,6},{10,... | collective-permute-start | bytes 18440 | tf_op jit(solution)/shard_map/ppermute | solution.py:257
  59.2 5.5 %collective-permute-start.5 = (f32[2,384]{1,0:T(2,128)S(1)}, f32[2,384]{1,0:T(2,128)S(1)}, u32[]{:S(2)}, u32[]{:S(2)}) collective-permute-start(f32[2,384]{1,0:T(2,128)S(1)} %get-tuple-element.46), channel_id=1, source_target_pairs={{0,28},{1,29},{2,30},{3,31},{4,0},{5,1},{6,2},{7,3},{8,4},{9,5},{1... | collective-permute-start | bytes 9224 | tf_op jit(solution)/shard_map/ppermute | solution.py:257
  72.9 3.6 %copy-start.1 = (bf16[384,768]{1,0:T(8,128)(2,1)S(1)}, bf16[384,768]{1,0:T(8,128)(2,1)}, u32[]{:S(2)}) copy-start(bf16[384,768]{1,0:T(8,128)(2,1)} %pre_txt.3) | copy-start | bytes 1769476
  74.6 19.7 %collective-permute-start.10 = (bf16[384,768]{1,0:T(8,128)(2,1)}, bf16[384,768]{1,0:T(8,128)(2,1)}, u32[]{:S(2)}, u32[]{:S(2)}) collective-permute-start(bf16[384,768]{1,0:T(8,128)(2,1)} %get-tuple-element.63), channel_id=1, source_target_pairs={{0,1},{1,0},{2,3},{3,2},{4,5},{5,4},{6,7},{7,6},{8,9},{9,8},{10,11... | collective-permute-start | bytes 1769480 | tf_op jit(solution)/shard_map/ppermute | solution.py:257
  76.5 4.9 %copy-start.3 = (bf16[384,768]{1,0:T(8,128)(2,1)S(1)}, bf16[384,768]{1,0:T(8,128)(2,1)}, u32[]{:S(2)}) copy-start(bf16[384,768]{1,0:T(8,128)(2,1)} %pre_img.3) | copy-start | bytes 1769476
  76.5 4.9 %copy-start.5 = (bf16[384,768]{1,0:T(8,128)(2,1)S(1)}, bf16[384,768]{1,0:T(8,128)(2,1)}, u32[]{:S(2)}) copy-start(bf16[384,768]{1,0:T(8,128)(2,1)} %copy-done.4) | copy-start | bytes 1769476
  77.9 6.4 %copy-start.7 = (bf16[384,768]{1,0:T(8,128)(2,1)S(1)}, bf16[384,768]{1,0:T(8,128)(2,1)}, u32[]{:S(2)}) copy-start(bf16[384,768]{1,0:T(8,128)(2,1)} %copy-done.6) | copy-start | bytes 1769476
  78.0 6.4 %copy-start.9 = (f32[384,384]{1,0:T(8,128)S(1)}, f32[384,384]{1,0:T(8,128)}, u32[]{:S(2)}) copy-start(f32[384,384]{1,0:T(8,128)} %copy-done.8) | copy-start | bytes 1769476
  78.0 6.3 %collective-permute-start.9 = (f32[1,384]{1,0:T(1,128)S(1)}, f32[1,384]{1,0:T(1,128)S(1)}, u32[]{:S(2)}, u32[]{:S(2)}) collective-permute-start(f32[1,384]{1,0:T(1,128)S(1)} %get-tuple-element.59), channel_id=1, source_target_pairs={{0,480},{1,481},{2,482},{3,483},{4,484},{5,485},{6,486},{7,487},{8... | collective-permute-start | bytes 4616 | tf_op jit(solution)/shard_map/ppermute | solution.py:257

commit v3 on v2

--- a/solution.py
+++ b/solution.py
@@ -66,8 +66,12 @@
 
 
 def pack(out, part, stats):
-    rows, width = part.shape
-    out[:rows, :] = part.astype(BF16)
+    out[: part.shape[0], :] = part.astype(BF16)
+    pack_tail(out, part.shape[0], stats)
+
+
+def pack_tail(out, rows, stats):
+    width = out.shape[1]
     place = lax.broadcasted_iota(jnp.int32, (TAIL, rows), 0)
     tail = jnp.zeros((TAIL, rows), F32)
     spot = 0
@@ -147,19 +151,21 @@
 
 
 def late_kernel(image_x, text, text_p, stat_v, s_xt, s_xp, stat_x, packed):
-    img = image_x[...]
-    first = scores_t(text[...], img)
-    second = scores_t(text_p[...], img)
-    s_xt[...] = first
-    s_xp[...] = second
-    peak = peak_of(first, second)
-    first = jnp.exp(first - peak)
-    second = jnp.exp(second - peak)
-    total = total_of(first) + total_of(second)
-    part = image_term(first, text[...]) + image_term(second, text_p[...])
-    pack(packed, part, (peak, total) + pair(stat_v))
-    stat_x[0:1, :] = peak
-    stat_x[1:2, :] = total
+    rows = text.shape[0]
+    for low, high in ((0, 256), (256, rows)):
+        img = image_x[low:high, :]
+        first = scores_t(text[...], img)
+        second = scores_t(text_p[...], img)
+        s_xt[:, low:high] = first
+        s_xp[:, low:high] = second
+        peak = peak_of(first, second)
+        first = jnp.exp(first - peak)
+        second = jnp.exp(second - peak)
+        part = image_term(first, text[...]) + image_term(second, text_p[...])
+        packed[low:high, :] = part.astype(BF16)
+        stat_x[0:1, low:high] = peak
+        stat_x[1:2, low:high] = total_of(first) + total_of(second)
+    pack_tail(packed, rows, pair(stat_x) + pair(stat_v))
 
 
 def lse_kernel(
@@ -223,10 +229,6 @@
     text_all[...] = text_sum[...] + text_term(jnp.exp(s_h[...] - lse_h[...]), image_h[...])
 
 
-def last_kernel(text_all, slope, got_p, grad_txt):
-    grad_txt[...] = (text_all[...] + got_p[...].astype(F32)) * slope[...]
-
-
 def together(*arrays):
     return lax.optimization_barrier(arrays)
 
@@ -336,7 +338,7 @@
         (text_all,) = run(
             more_kernel, (wide,), text_sum, lse_h, s_h, image_h, matmuls=1, name="more"
         )
-        (grad_txt,) = run(last_kernel, (wide,), text_all, slope, got_p, name="last")
+        grad_txt = (text_all + got_p.astype(F32)) * slope
         return grad_img, grad_txt, row_loss.reshape(rows)
 
     in_specs = (P(AXES, None), P(AXES, None))

time: 97 us -> 97.7 us (level)
  other arithmetic: 0.6 us -> 2.89 us
  Pallas kernels: 13.6 us -> 11.8 us
    mul x0 -> x1, other arithmetic: none -> 2.29 us  [per_device(): grad_txt = (text_all + got_p.astype(F32)) * slope]
    pallas_call x10 -> x9, Pallas kernels: 13.6 us -> 11.8 us  [run(): pl.pallas_call(kernel, out_shape=outs, in_specs=[smem if v.dtype == jnp.i...]
where the time goes in v3:
time: 97.7 us; the launch traced here: 97.1 us
  starting transfers between devices  53.7 us (55%)
  waiting for transfers between devices  25.7 us (26%)
  Pallas kernels  11.8 us (12%)
  other arithmetic  2.89 us (3%)
  local copies, waits for them, and re-layouts  2.16 us (2%)
    ppermute x11, starting transfers between devices, send(): return lax.ppermute(array, AXES, plan)  53.7 us
    ppermute x11, waiting for transfers between devices, send(): return lax.ppermute(array, AXES, plan)  25.7 us
    pallas_call x9, Pallas kernels, run(): pl.pallas_call(kernel, out_shape=outs, in_specs=[smem if v.dtype == jnp.i...  11.8 us
    mul x1, other arithmetic, per_device(): grad_txt = (text_all + got_p.astype(F32)) * slope  2.29 us
    unnamed x20, local copies, waits for them, and re-layouts  2.16 us
  transfers between devices with their start and end apart: 11, of which 5 were waited for; matrix products, arithmetic and copies ran while one was open for 1% of the time, Pallas kernels for 10%

profile of v3, /device:TPU:6, one launch (start us, length us, event | category | flops | bytes accessed | tf_op | source)
XLA Modules:
  0.0 97.1 jit_solution(10650298545493912898)
XLA Ops:
  0.6 6.1 %collective-permute-start = (bf16[384,768]{1,0:T(8,128)(2,1)}, bf16[384,768]{1,0:T(8,128)(2,1)S(1)}, u32[]{:S(2)}, u32[]{:S(2)}) collective-permute-start(bf16[384,768]{1,0:T(8,128)(2,1)} %pre_txt.3), channel_id=1, source_target_pairs={{0,1},{1,0},{2,3},{3,2},{4,5},{5,4},{6,7},{7,6},{8,9},{9,8},{10,11... | collective-permute-start | bytes 1769480 | tf_op jit(solution)/shard_map/ppermute | solution.py:259
  6.7 5.4 %collective-permute-start.1 = (bf16[384,768]{1,0:T(8,128)(2,1)}, bf16[384,768]{1,0:T(8,128)(2,1)S(1)}, u32[]{:S(2)}, u32[]{:S(2)}) collective-permute-start(bf16[384,768]{1,0:T(8,128)(2,1)} %pre_img.3), channel_id=1, source_target_pairs={{0,28},{1,29},{2,30},{3,31},{4,0},{5,1},{6,2},{7,3},{8,4},{9,5},{1... | collective-permute-start | bytes 1769480 | tf_op jit(solution)/shard_map/ppermute | solution.py:259
  12.1 7.3 %collective-permute-start.3 = (bf16[384,768]{1,0:T(8,128)(2,1)}, bf16[384,768]{1,0:T(8,128)(2,1)S(1)}, u32[]{:S(2)}, u32[]{:S(2)}) collective-permute-start(bf16[384,768]{1,0:T(8,128)(2,1)} %pre_img.3), channel_id=1, source_target_pairs={{0,480},{1,481},{2,482},{3,483},{4,484},{5,485},{6,486},{7,487},{8... | collective-permute-start | bytes 1769480 | tf_op jit(solution)/shard_map/ppermute | solution.py:259
  19.4 1.1 %copy-done = bf16[384,768]{1,0:T(8,128)(2,1)S(1)} copy-done((bf16[384,768]{1,0:T(8,128)(2,1)S(1)}, bf16[384,768]{1,0:T(8,128)(2,1)}, u32[]{:S(2)}) %copy-start) | copy-done | bytes 589848
  20.4 1.1 %copy-done.2 = bf16[384,768]{1,0:T(8,128)(2,1)S(1)} copy-done((bf16[384,768]{1,0:T(8,128)(2,1)S(1)}, bf16[384,768]{1,0:T(8,128)(2,1)}, u32[]{:S(2)}) %copy-start.2) | copy-done | bytes 589848
  22.6 11.1 %collective-permute-start.2 = (bf16[384,768]{1,0:T(8,128)(2,1)S(1)}, bf16[384,768]{1,0:T(8,128)(2,1)S(1)}, u32[]{:S(2)}, u32[]{:S(2)}) collective-permute-start(bf16[384,768]{1,0:T(8,128)(2,1)S(1)} %get-tuple-element.38.image), channel_id=1, source_target_pairs={{0,31},{1,30},{2,1},{3,0},{4,3},{5,2},{6,5},{7,4},{8,7},{9,6},{10,... | collective-permute-start | bytes 1769480 | tf_op jit(solution)/shard_map/ppermute | solution.py:259
  33.8 2.4 %early.1 = (bf16[384,768]{1,0:T(8,128)(2,1)S(1)}, bf16[384,768]{1,0:T(8,128)(2,1)S(1)}, f32[384,384]{1,0:T(8,128)S(1)}, f32[384,384]{1,0:T(8,128)S(1)}, f32[384,...) custom-call(s32[1]{0:T(128)} %bitcast.even, ...), custom_call_target="tpu_custom_call" | custom-call | flops 1132462080 | tf_op jit(solution)/shard_map/early/pallas_call | solution.py:264
  36.2 1.9 %collective-permute-start.8 = (bf16[400,768]{1,0:T(8,128)(2,1)S(1)}, bf16[400,768]{1,0:T(8,128)(2,1)S(1)}, u32[]{:S(2)}, u32[]{:S(2)}) collective-permute-start(bf16[400,768]{1,0:T(8,128)(2,1)S(1)} %get-tuple-element.48), channel_id=1, source_target_pairs={{28,0},{29,1},{30,2},{31,3},{0,4},{1,5},{2,6},{3,7},{4,8},{5,9},{6... | collective-permute-start | bytes 1843208 | tf_op jit(solution)/shard_map/ppermute | solution.py:259
  38.1 1.1 %hop.1 = (bf16[384,768]{1,0:T(8,128)(2,1)S(1)}, f32[384,384]{1,0:T(8,128)S(1)}, bf16[400,768]{1,0:T(8,128)(2,1)S(1)}) custom-call(bf16[384,768]{1,0:T(8,128)(2,1)S(1)} %get-tuple-element.35.text, bf16[384,768]{1,0:T(8,128)(2,1)S(1)} %collective-permute-done.3.pre_hop), custom_call_target="tpu_custom_call" | custom-call | flops 452984832 | tf_op jit(solution)/shard_map/hop/pallas_call | solution.py:264
  39.2 1.9 %collective-permute-start.4 = (bf16[400,768]{1,0:T(8,128)(2,1)S(1)}, bf16[400,768]{1,0:T(8,128)(2,1)S(1)}, u32[]{:S(2)}, u32[]{:S(2)}) collective-permute-start(bf16[400,768]{1,0:T(8,128)(2,1)S(1)} %get-tuple-element.44), channel_id=1, source_target_pairs={{480,0},{481,1},{482,2},{483,3},{484,4},{485,5},{486,6},{487,7},{4... | collective-permute-start | bytes 1843208 | tf_op jit(solution)/shard_map/ppermute | solution.py:259
  41.1 4.1 %collective-permute-done.2.image_x = bf16[384,768]{1,0:T(8,128)(2,1)S(1)} collective-permute-done((bf16[384,768]{1,0:T(8,128)(2,1)S(1)}, bf16[384,768]{1,0:T(8,128)(2,1)S(1)}, u32[]{:S(2)}, u32[]{:S(2)}) %collective-permute-start.2) | collective-permute-done | bytes 589856 | tf_op jit(solution)/shard_map/ppermute | solution.py:259
  45.2 2.3 %late.1 = (f32[384,384]{1,0:T(8,128)S(1)}, f32[384,384]{1,0:T(8,128)S(1)}, f32[2,384]{1,0:T(2,128)S(1)}, bf16[400,768]{1,0:T(8,128)(2,1)S(1)}) custom-call(bf16[384,768]{1,0:T(8,128)(2,1)S(1)} %collective-permute-done.2.image_x, bf16[384,768]{1,0:T(8,128)(2,1)S(1)} %get-tuple-element.35.text, bf16[384,768]{1,0:T(8,128)(2,1)S(1)} %get-tuple-element.40.text_p, ...), custom_call_target="tpu_custom_call" | custom-call | flops 905969664 | tf_op jit(solution)/shard_map/late/pallas_call | solution.py:264
  47.5 6.0 %collective-permute-start.7 = (bf16[400,768]{1,0:T(8,128)(2,1)S(1)}, bf16[400,768]{1,0:T(8,128)(2,1)S(1)}, u32[]{:S(2)}, u32[]{:S(2)}) collective-permute-start(bf16[400,768]{1,0:T(8,128)(2,1)S(1)} %get-tuple-element.47), channel_id=1, source_target_pairs={{31,0},{30,1},{1,2},{0,3},{3,4},{2,5},{5,6},{4,7},{7,8},{6,9},{9,1... | collective-permute-start | bytes 1843208 | tf_op jit(solution)/shard_map/ppermute | solution.py:259
  53.5 6.1 %collective-permute-start.6 = (f32[4,384]{1,0:T(4,128)S(1)}, f32[4,384]{1,0:T(4,128)S(1)}, u32[]{:S(2)}, u32[]{:S(2)}) collective-permute-start(f32[4,384]{1,0:T(4,128)S(1)} %get-tuple-element.45.stat_c), channel_id=1, source_target_pairs={{0,31},{1,30},{2,1},{3,0},{4,3},{5,2},{6,5},{7,4},{8,7},{9,6},{10,... | collective-permute-start | bytes 18440 | tf_op jit(solution)/shard_map/ppermute | solution.py:259
  59.7 2.5 %collective-permute-start.5 = (f32[2,384]{1,0:T(2,128)S(1)}, f32[2,384]{1,0:T(2,128)S(1)}, u32[]{:S(2)}, u32[]{:S(2)}) collective-permute-start(f32[2,384]{1,0:T(2,128)S(1)} %get-tuple-element.46), channel_id=1, source_target_pairs={{0,28},{1,29},{2,30},{3,31},{4,0},{5,1},{6,2},{7,3},{8,4},{9,5},{1... | collective-permute-start | bytes 9224 | tf_op jit(solution)/shard_map/ppermute | solution.py:259
  62.2 3.0 %collective-permute-done.5.from_i = f32[2,384]{1,0:T(2,128)S(1)} collective-permute-done((f32[2,384]{1,0:T(2,128)S(1)}, f32[2,384]{1,0:T(2,128)S(1)}, u32[]{:S(2)}, u32[]{:S(2)}) %collective-permute-start.5) | collective-permute-done | bytes 3104 | tf_op jit(solution)/shard_map/ppermute | solution.py:259
  65.2 8.3 %collective-permute-done.7.home_x = bf16[400,768]{1,0:T(8,128)(2,1)S(1)} collective-permute-done((bf16[400,768]{1,0:T(8,128)(2,1)S(1)}, bf16[400,768]{1,0:T(8,128)(2,1)S(1)}, u32[]{:S(2)}, u32[]{:S(2)}) %collective-permute-start.7) | collective-permute-done | bytes 614432 | tf_op jit(solution)/shard_map/ppermute | solution.py:259
  73.4 1.7 %lse.1 = (bf16[384,768]{1,0:T(8,128)(2,1)}, f32[1,384]{1,0:T(1,128)S(1)}, f32[2,384]{1,0:T(2,128)S(1)}) custom-call(s32[1]{0:T(128)} %bitcast.even, f32[4,384]{1,0:T(4,128)S(1)} %get-tuple-element.45.stat_c, f32[2,384]{1,0:T(2,128)S(1)} %get-tuple-element.41.stat_v, f32[2,384]{1,0:T(2,128)S(1)} %collective-permute-done.5.from_i, ...), custom_call_target="tpu_custom_call" | custom-call | flops 452984832 | tf_op jit(solution)/shard_map/lse/pallas_call | solution.py:264
  75.1 1.9 %collective-permute-start.10 = (bf16[384,768]{1,0:T(8,128)(2,1)}, bf16[384,768]{1,0:T(8,128)(2,1)}, u32[]{:S(2)}, u32[]{:S(2)}) collective-permute-start(bf16[384,768]{1,0:T(8,128)(2,1)} %get-tuple-element.62), channel_id=1, source_target_pairs={{0,1},{1,0},{2,3},{3,2},{4,5},{5,4},{6,7},{7,6},{8,9},{9,8},{10,11... | collective-permute-start | bytes 1769480 | tf_op jit(solution)/shard_map/ppermute | solution.py:259
  77.0 1.4 %text.1 = (f32[384,768]{1,0:T(8,128)S(1)}, f32[384,768]{1,0:T(8,128)S(1)}, f32[1,384]{1,0:T(1,128)S(1)}) custom-call(bf16[384,768]{1,0:T(8,128)(2,1)S(1)} %copy-done.1, f32[1,384]{1,0:T(1,128)S(1)} %get-tuple-element.52.lse_i, f32[2,384]{1,0:T(2,128)S(1)} %get-tuple-element.55.lse_xv, f32[384,384]{1,0:T(8,128)S(1)} %get-tuple-element.53.s_own, ...), custom_call_target="tpu_custom_call" | custom-call | flops 679477248 | tf_op jit(solution)/shard_map/text/pallas_call | solution.py:264
  78.4 3.5 %collective-permute-start.9 = (f32[1,384]{1,0:T(1,128)S(1)}, f32[1,384]{1,0:T(1,128)S(1)}, u32[]{:S(2)}, u32[]{:S(2)}) collective-permute-start(f32[1,384]{1,0:T(1,128)S(1)} %get-tuple-element.59), channel_id=1, source_target_pairs={{0,480},{1,481},{2,482},{3,483},{4,484},{5,485},{6,486},{7,487},{8... | collective-permute-start | bytes 4616 | tf_op jit(solution)/shard_map/ppermute | solution.py:259
  82.0 2.2 %image.1 = (f32[384,768]{1,0:T(8,128)}, f32[1,384]{1,0:T(1,128)S(1)}) custom-call(s32[1]{0:T(128)} %bitcast.even, bf16[384,768]{1,0:T(8,128)(2,1)S(1)} %copy-done.3, f32[1,384]{1,0:T(1,128)S(1)} %get-tuple-element.52.lse_i, f32[384,384]{1,0:T(8,128)S(1)} %get-tuple-element.53.s_own, f32[384,384]{1,0:T(8,128)S(1)} %get-tuple-element.50.s_y, ...), custom_call_target="tpu_custom_call" | custom-call | flops 452984832 | tf_op jit(solution)/shard_map/image/pallas_call | solution.py:264
  85.2 9.6 %collective-permute-done.10 = bf16[384,768]{1,0:T(8,128)(2,1)} collective-permute-done((bf16[384,768]{1,0:T(8,128)(2,1)}, bf16[384,768]{1,0:T(8,128)(2,1)}, u32[]{:S(2)}, u32[]{:S(2)}) %collective-permute-start.10) | collective-permute-done | bytes 589856 | tf_op jit(solution)/shard_map/ppermute | solution.py:259
  94.8 2.3 %add_multiply_fusion = f32[384,768]{1,0:T(8,128)} fusion(f32[384,768]{1,0:T(8,128)S(1)} %get-tuple-element.63, f32[384,768]{1,0:T(8,128)S(1)} %more.1, bf16[384,768]{1,0:T(8,128)(2,1)} %collective-permute-done.10), kind=kLoop, calls=%fused_computation | loop fusion | flops 884736 | bytes 4128768 | tf_op jit(solution)/shard_map/mul | solution.py:341
  (29 shorter events, 2.2 us)
Async XLA Ops:
  0.6 22.0 %collective-permute-start = (bf16[384,768]{1,0:T(8,128)(2,1)}, bf16[384,768]{1,0:T(8,128)(2,1)S(1)}, u32[]{:S(2)}, u32[]{:S(2)}) collective-permute-start(bf16[384,768]{1,0:T(8,128)(2,1)} %pre_txt.3), channel_id=1, source_target_pairs={{0,1},{1,0},{2,3},{3,2},{4,5},{5,4},{6,7},{7,6},{8,9},{9,8},{10,11... | collective-permute-start | bytes 1769480 | tf_op jit(solution)/shard_map/ppermute | solution.py:259
  6.7 27.0 %collective-permute-start.1 = (bf16[384,768]{1,0:T(8,128)(2,1)}, bf16[384,768]{1,0:T(8,128)(2,1)S(1)}, u32[]{:S(2)}, u32[]{:S(2)}) collective-permute-start(bf16[384,768]{1,0:T(8,128)(2,1)} %pre_img.3), channel_id=1, source_target_pairs={{0,28},{1,29},{2,30},{3,31},{4,0},{5,1},{6,2},{7,3},{8,4},{9,5},{1... | collective-permute-start | bytes 1769480 | tf_op jit(solution)/shard_map/ppermute | solution.py:259
  12.1 24.0 %collective-permute-start.3 = (bf16[384,768]{1,0:T(8,128)(2,1)}, bf16[384,768]{1,0:T(8,128)(2,1)S(1)}, u32[]{:S(2)}, u32[]{:S(2)}) collective-permute-start(bf16[384,768]{1,0:T(8,128)(2,1)} %pre_img.3), channel_id=1, source_target_pairs={{0,480},{1,481},{2,482},{3,483},{4,484},{5,485},{6,486},{7,487},{8... | collective-permute-start | bytes 1769480 | tf_op jit(solution)/shard_map/ppermute | solution.py:259
  19.4 1.1 %copy-start = (bf16[384,768]{1,0:T(8,128)(2,1)S(1)}, bf16[384,768]{1,0:T(8,128)(2,1)}, u32[]{:S(2)}) copy-start(bf16[384,768]{1,0:T(8,128)(2,1)} %pre_txt.3) | copy-start | bytes 1769476
  20.4 1.1 %copy-start.2 = (bf16[384,768]{1,0:T(8,128)(2,1)S(1)}, bf16[384,768]{1,0:T(8,128)(2,1)}, u32[]{:S(2)}) copy-start(bf16[384,768]{1,0:T(8,128)(2,1)} %pre_img.3) | copy-start | bytes 1769476
  21.8 23.3 %copy-start.4 = (bf16[384,768]{1,0:T(8,128)(2,1)}, bf16[384,768]{1,0:T(8,128)(2,1)S(1)}, u32[]{:S(2)}) copy-start(bf16[384,768]{1,0:T(8,128)(2,1)S(1)} %get-tuple-element.35.text) | copy-start | bytes 1769476
  22.6 22.6 %collective-permute-start.2 = (bf16[384,768]{1,0:T(8,128)(2,1)S(1)}, bf16[384,768]{1,0:T(8,128)(2,1)S(1)}, u32[]{:S(2)}, u32[]{:S(2)}) collective-permute-start(bf16[384,768]{1,0:T(8,128)(2,1)S(1)} %get-tuple-element.38.image), channel_id=1, source_target_pairs={{0,31},{1,30},{2,1},{3,0},{4,3},{5,2},{6,5},{7,4},{8,7},{9,6},{10,... | collective-permute-start | bytes 1769480 | tf_op jit(solution)/shard_map/ppermute | solution.py:259
  36.2 26.0 %collective-permute-start.8 = (bf16[400,768]{1,0:T(8,128)(2,1)S(1)}, bf16[400,768]{1,0:T(8,128)(2,1)S(1)}, u32[]{:S(2)}, u32[]{:S(2)}) collective-permute-start(bf16[400,768]{1,0:T(8,128)(2,1)S(1)} %get-tuple-element.48), channel_id=1, source_target_pairs={{28,0},{29,1},{30,2},{31,3},{0,4},{1,5},{2,6},{3,7},{4,8},{5,9},{6... | collective-permute-start | bytes 1843208 | tf_op jit(solution)/shard_map/ppermute | solution.py:259
  39.2 8.4 %copy-start.6 = (bf16[384,768]{1,0:T(8,128)(2,1)}, bf16[384,768]{1,0:T(8,128)(2,1)S(1)}, u32[]{:S(2)}) copy-start(bf16[384,768]{1,0:T(8,128)(2,1)S(1)} %get-tuple-element.61.image_h) | copy-start | bytes 1769476
  39.2 8.4 %copy-start.8 = (f32[384,384]{1,0:T(8,128)}, f32[384,384]{1,0:T(8,128)S(1)}, u32[]{:S(2)}) copy-start(f32[384,384]{1,0:T(8,128)S(1)} %get-tuple-element.60.s_h) | copy-start | bytes 1769476
  39.2 14.3 %collective-permute-start.4 = (bf16[400,768]{1,0:T(8,128)(2,1)S(1)}, bf16[400,768]{1,0:T(8,128)(2,1)S(1)}, u32[]{:S(2)}, u32[]{:S(2)}) collective-permute-start(bf16[400,768]{1,0:T(8,128)(2,1)S(1)} %get-tuple-element.44), channel_id=1, source_target_pairs={{480,0},{481,1},{482,2},{483,3},{484,4},{485,5},{486,6},{487,7},{4... | collective-permute-start | bytes 1843208 | tf_op jit(solution)/shard_map/ppermute | solution.py:259
  47.5 25.9 %collective-permute-start.7 = (bf16[400,768]{1,0:T(8,128)(2,1)S(1)}, bf16[400,768]{1,0:T(8,128)(2,1)S(1)}, u32[]{:S(2)}, u32[]{:S(2)}) collective-permute-start(bf16[400,768]{1,0:T(8,128)(2,1)S(1)} %get-tuple-element.47), channel_id=1, source_target_pairs={{31,0},{30,1},{1,2},{0,3},{3,4},{2,5},{5,6},{4,7},{7,8},{6,9},{9,1... | collective-permute-start | bytes 1843208 | tf_op jit(solution)/shard_map/ppermute | solution.py:259
  53.5 11.6 %collective-permute-start.6 = (f32[4,384]{1,0:T(4,128)S(1)}, f32[4,384]{1,0:T(4,128)S(1)}, u32[]{:S(2)}, u32[]{:S(2)}) collective-permute-start(f32[4,384]{1,0:T(4,128)S(1)} %get-tuple-element.45.stat_c), channel_id=1, source_target_pairs={{0,31},{1,30},{2,1},{3,0},{4,3},{5,2},{6,5},{7,4},{8,7},{9,6},{10,... | collective-permute-start | bytes 18440 | tf_op jit(solution)/shard_map/ppermute | solution.py:259
  59.7 5.5 %collective-permute-start.5 = (f32[2,384]{1,0:T(2,128)S(1)}, f32[2,384]{1,0:T(2,128)S(1)}, u32[]{:S(2)}, u32[]{:S(2)}) collective-permute-start(f32[2,384]{1,0:T(2,128)S(1)} %get-tuple-element.46), channel_id=1, source_target_pairs={{0,28},{1,29},{2,30},{3,31},{4,0},{5,1},{6,2},{7,3},{8,4},{9,5},{1... | collective-permute-start | bytes 9224 | tf_op jit(solution)/shard_map/ppermute | solution.py:259
  73.4 3.6 %copy-start.1 = (bf16[384,768]{1,0:T(8,128)(2,1)S(1)}, bf16[384,768]{1,0:T(8,128)(2,1)}, u32[]{:S(2)}) copy-start(bf16[384,768]{1,0:T(8,128)(2,1)} %pre_txt.3) | copy-start | bytes 1769476
  75.1 19.7 %collective-permute-start.10 = (bf16[384,768]{1,0:T(8,128)(2,1)}, bf16[384,768]{1,0:T(8,128)(2,1)}, u32[]{:S(2)}, u32[]{:S(2)}) collective-permute-start(bf16[384,768]{1,0:T(8,128)(2,1)} %get-tuple-element.62), channel_id=1, source_target_pairs={{0,1},{1,0},{2,3},{3,2},{4,5},{5,4},{6,7},{7,6},{8,9},{9,8},{10,11... | collective-permute-start | bytes 1769480 | tf_op jit(solution)/shard_map/ppermute | solution.py:259
  77.0 4.9 %copy-start.3 = (bf16[384,768]{1,0:T(8,128)(2,1)S(1)}, bf16[384,768]{1,0:T(8,128)(2,1)}, u32[]{:S(2)}) copy-start(bf16[384,768]{1,0:T(8,128)(2,1)} %pre_img.3) | copy-start | bytes 1769476
  77.0 4.9 %copy-start.5 = (bf16[384,768]{1,0:T(8,128)(2,1)S(1)}, bf16[384,768]{1,0:T(8,128)(2,1)}, u32[]{:S(2)}) copy-start(bf16[384,768]{1,0:T(8,128)(2,1)} %copy-done.4) | copy-start | bytes 1769476
  78.4 6.3 %copy-start.7 = (bf16[384,768]{1,0:T(8,128)(2,1)S(1)}, bf16[384,768]{1,0:T(8,128)(2,1)}, u32[]{:S(2)}) copy-start(bf16[384,768]{1,0:T(8,128)(2,1)} %copy-done.6) | copy-start | bytes 1769476
  78.4 6.3 %copy-start.9 = (f32[384,384]{1,0:T(8,128)S(1)}, f32[384,384]{1,0:T(8,128)}, u32[]{:S(2)}) copy-start(f32[384,384]{1,0:T(8,128)} %copy-done.8) | copy-start | bytes 1769476
  78.4 6.3 %collective-permute-start.9 = (f32[1,384]{1,0:T(1,128)S(1)}, f32[1,384]{1,0:T(1,128)S(1)}, u32[]{:S(2)}, u32[]{:S(2)}) collective-permute-start(f32[1,384]{1,0:T(1,128)S(1)} %get-tuple-element.59), channel_id=1, source_target_pairs={{0,480},{1,481},{2,482},{3,483},{4,484},{5,485},{6,486},{7,487},{8... | collective-permute-start | bytes 4616 | tf_op jit(solution)/shard_map/ppermute | solution.py:259

commit v4 on v2

--- a/solution.py
+++ b/solution.py
@@ -90,7 +90,7 @@
     return row(6 * spot), row(6 * spot + 3)
 
 
-def hop_kernel(text, pre_hop, image_h, s_h, packed):
+def hop_kernel(even, text, image_o, s_y, pre_hop, image_h, s_h, s_own, stat_o, packed):
     image = soft_of(pre_hop).astype(BF16)
     image_h[...] = image
     scores = scores_t(text[...], image)
@@ -98,6 +98,12 @@
     peak = peak_of(scores)
     weights = jnp.exp(scores - peak)
     pack(packed, image_term(weights, text[...]), (peak, total_of(weights)))
+    so = scores_t(text[...], image_o[...])
+    s_own[...] = so
+    sy_o = jnp.where(even[0] == 1, LOW, s_y[...])
+    peak = peak_of(so, sy_o)
+    stat_o[0:1, :] = peak
+    stat_o[1:2, :] = total_of(jnp.exp(so - peak)) + total_of(jnp.exp(sy_o - peak))
 
 
 def soft_kernel(pre_img, pre_txt, image, text):
@@ -107,7 +113,7 @@
 
 def early_kernel(
     even, image, text, pre_p, pre_v,
-    text_p, image_v, s_own, s_v, s_y, stat_v, stat_o, packed,
+    text_p, image_v, s_v, s_y, stat_v, packed,
 ):
     is_even = even[0] == 1
     img = image[...]
@@ -128,12 +134,6 @@
     stat_v[0:1, :] = peak
     stat_v[1:2, :] = total
     pack(packed, image_term(first, txt) + image_term(second, other), (peak, total))
-    so = scores_t(txt, img)
-    s_own[...] = so
-    sy_o = jnp.where(is_even, LOW, sy)
-    peak = peak_of(so, sy_o)
-    stat_o[0:1, :] = peak
-    stat_o[1:2, :] = total_of(jnp.exp(so - peak)) + total_of(jnp.exp(sy_o - peak))
 
 
 def home_kernel(stat_o, stat_x, home_h, stat_i, stat_c):
@@ -291,15 +291,17 @@
         pre_p, img_x = together(pre_p, image)
         image_x = send(img_x, cross)
 
-        text_p, image_v, s_own, s_v, s_y, stat_v, stat_o, part_v = run(
+        text_p, image_v, s_v, s_y, stat_v, part_v = run(
             early_kernel,
-            (block, block, square, square, square, stat(2), stat(2), packed),
-            even, image, text, pre_p, pre_v, matmuls=5, name="early",
+            (block, block, square, square, stat(2), packed),
+            even, image, text, pre_p, pre_v, matmuls=4, name="early",
         )
         home_v = send(part_v, forth)
         text_p, pre_h = together(text_p, pre_h)
-        image_h, s_h, part_h = run(
-            hop_kernel, (block, square, packed), text, pre_h, matmuls=2, name="hop"
+        image_h, s_h, s_own, stat_o, part_h = run(
+            hop_kernel,
+            (block, square, square, stat(2), packed),
+            even, text, image, s_y, pre_h, matmuls=3, name="hop",
         )
         home_h = send(part_h, hop)
         s_xt, s_xp, stat_x, part_x = run(

time: 97 us -> 97 us (level)
  waiting for transfers between devices: 25.6 us -> 24.5 us
    ppermute x11, waiting for transfers between devices: 25.6 us -> 24.5 us  [send(): return lax.ppermute(array, AXES, plan)]
where the time goes in v4:
time: 97 us; the launch traced here: 96.5 us
  starting transfers between devices  53.8 us (55%)
  waiting for transfers between devices  24.5 us (25%)
  Pallas kernels  13.7 us (14%)
  local copies, waits for them, and re-layouts  2.98 us (3%)
    ppermute x11, starting transfers between devices, send(): return lax.ppermute(array, AXES, plan)  53.8 us
    ppermute x11, waiting for transfers between devices, send(): return lax.ppermute(array, AXES, plan)  24.5 us
    pallas_call x10, Pallas kernels, run(): pl.pallas_call(kernel, out_shape=outs, in_specs=[smem if v.dtype == jnp.i...  13.7 us
    unnamed x20, local copies, waits for them, and re-layouts  2.98 us
  transfers between devices with their start and end apart: 11, of which 5 were waited for; matrix products, arithmetic and copies ran while one was open for 1% of the time, Pallas kernels for 10%

profile of v4, /device:TPU:6, one launch (start us, length us, event | category | flops | bytes accessed | tf_op | source)
XLA Modules:
  0.0 96.5 jit_solution(12902541957679858786)
XLA Ops:
  0.6 6.1 %collective-permute-start = (bf16[384,768]{1,0:T(8,128)(2,1)}, bf16[384,768]{1,0:T(8,128)(2,1)S(1)}, u32[]{:S(2)}, u32[]{:S(2)}) collective-permute-start(bf16[384,768]{1,0:T(8,128)(2,1)} %pre_txt.3), channel_id=1, source_target_pairs={{0,1},{1,0},{2,3},{3,2},{4,5},{5,4},{6,7},{7,6},{8,9},{9,8},{10,11... | collective-permute-start | bytes 1769480 | tf_op jit(solution)/shard_map/ppermute | solution.py:257
  6.7 5.4 %collective-permute-start.1 = (bf16[384,768]{1,0:T(8,128)(2,1)}, bf16[384,768]{1,0:T(8,128)(2,1)S(1)}, u32[]{:S(2)}, u32[]{:S(2)}) collective-permute-start(bf16[384,768]{1,0:T(8,128)(2,1)} %pre_img.3), channel_id=1, source_target_pairs={{0,28},{1,29},{2,30},{3,31},{4,0},{5,1},{6,2},{7,3},{8,4},{9,5},{1... | collective-permute-start | bytes 1769480 | tf_op jit(solution)/shard_map/ppermute | solution.py:257
  12.1 7.3 %collective-permute-start.2 = (bf16[384,768]{1,0:T(8,128)(2,1)}, bf16[384,768]{1,0:T(8,128)(2,1)S(1)}, u32[]{:S(2)}, u32[]{:S(2)}) collective-permute-start(bf16[384,768]{1,0:T(8,128)(2,1)} %pre_img.3), channel_id=1, source_target_pairs={{0,480},{1,481},{2,482},{3,483},{4,484},{5,485},{6,486},{7,487},{8... | collective-permute-start | bytes 1769480 | tf_op jit(solution)/shard_map/ppermute | solution.py:257
  19.4 1.1 %copy-done = bf16[384,768]{1,0:T(8,128)(2,1)S(1)} copy-done((bf16[384,768]{1,0:T(8,128)(2,1)S(1)}, bf16[384,768]{1,0:T(8,128)(2,1)}, u32[]{:S(2)}) %copy-start) | copy-done | bytes 589848
  20.4 1.1 %copy-done.2 = bf16[384,768]{1,0:T(8,128)(2,1)S(1)} copy-done((bf16[384,768]{1,0:T(8,128)(2,1)S(1)}, bf16[384,768]{1,0:T(8,128)(2,1)}, u32[]{:S(2)}) %copy-start.2) | copy-done | bytes 589848
  22.6 11.1 %collective-permute-start.3 = (bf16[384,768]{1,0:T(8,128)(2,1)S(1)}, bf16[384,768]{1,0:T(8,128)(2,1)S(1)}, u32[]{:S(2)}, u32[]{:S(2)}) collective-permute-start(bf16[384,768]{1,0:T(8,128)(2,1)S(1)} %get-tuple-element.41.image.image_o), channel_id=1, source_target_pairs={{0,31},{1,30},{2,1},{3,0},{4,3},{5,2},{6,5},{7,4},{8,7},{9,6},{10,... | collective-permute-start | bytes 1769480 | tf_op jit(solution)/shard_map/ppermute | solution.py:257
  33.8 1.9 %early.1 = (bf16[384,768]{1,0:T(8,128)(2,1)S(1)}, bf16[384,768]{1,0:T(8,128)(2,1)S(1)}, f32[384,384]{1,0:T(8,128)S(1)}, f32[384,384]{1,0:T(8,128)S(1)}, f32[2,38...) custom-call(s32[1]{0:T(128)} %bitcast.even, bf16[384,768]{1,0:T(8,128)(2,1)S(1)} %get-tuple-element.41.image.image_o, ...), custom_call_target="tpu_custom_call" | custom-call | flops 905969664 | tf_op jit(solution)/shard_map/early/pallas_call | solution.py:262
  35.7 1.9 %collective-permute-start.8 = (bf16[400,768]{1,0:T(8,128)(2,1)S(1)}, bf16[400,768]{1,0:T(8,128)(2,1)S(1)}, u32[]{:S(2)}, u32[]{:S(2)}) collective-permute-start(bf16[400,768]{1,0:T(8,128)(2,1)S(1)} %get-tuple-element.49), channel_id=1, source_target_pairs={{28,0},{29,1},{30,2},{31,3},{0,4},{1,5},{2,6},{3,7},{4,8},{5,9},{6... | collective-permute-start | bytes 1843208 | tf_op jit(solution)/shard_map/ppermute | solution.py:257
  37.6 1.6 %hop.1 = (bf16[384,768]{1,0:T(8,128)(2,1)S(1)}, f32[384,384]{1,0:T(8,128)S(1)}, f32[384,384]{1,0:T(8,128)S(1)}, f32[2,384]{1,0:T(2,128)S(1)}, bf16[400,768]{1,0:T(8,128)(2,1)S(1)}) custom-call(s32[1]{0:T(128)} %bitcast.even, bf16[384,768]{1,0:T(8,128)(2,1)S(1)} %get-tuple-element.34.text, bf16[384,768]{1,0:T(8,128)(2,1)S(1)} %get-tuple-element.41.image.image_o, ...), custom_call_target="tpu_custom_call" | custom-call | flops 679477248 | tf_op jit(solution)/shard_map/hop/pallas_call | solution.py:262
  40.1 2.0 %collective-permute-start.4 = (bf16[400,768]{1,0:T(8,128)(2,1)S(1)}, bf16[400,768]{1,0:T(8,128)(2,1)S(1)}, u32[]{:S(2)}, u32[]{:S(2)}) collective-permute-start(bf16[400,768]{1,0:T(8,128)(2,1)S(1)} %get-tuple-element.45), channel_id=1, source_target_pairs={{480,0},{481,1},{482,2},{483,3},{484,4},{485,5},{486,6},{487,7},{4... | collective-permute-start | bytes 1843208 | tf_op jit(solution)/shard_map/ppermute | solution.py:257
  42.2 3.0 %collective-permute-done.3.image_x = bf16[384,768]{1,0:T(8,128)(2,1)S(1)} collective-permute-done((bf16[384,768]{1,0:T(8,128)(2,1)S(1)}, bf16[384,768]{1,0:T(8,128)(2,1)S(1)}, u32[]{:S(2)}, u32[]{:S(2)}) %collective-permute-start.3) | collective-permute-done | bytes 589856 | tf_op jit(solution)/shard_map/ppermute | solution.py:257
  45.2 1.9 %late.1 = (f32[384,384]{1,0:T(8,128)S(1)}, f32[384,384]{1,0:T(8,128)S(1)}, f32[2,384]{1,0:T(2,128)S(1)}, bf16[400,768]{1,0:T(8,128)(2,1)S(1)}) custom-call(bf16[384,768]{1,0:T(8,128)(2,1)S(1)} %collective-permute-done.3.image_x, bf16[384,768]{1,0:T(8,128)(2,1)S(1)} %get-tuple-element.34.text, bf16[384,768]{1,0:T(8,128)(2,1)S(1)} %get-tuple-element.42.text_p, ...), custom_call_target="tpu_custom_call" | custom-call | flops 905969664 | tf_op jit(solution)/shard_map/late/pallas_call | solution.py:262
  47.1 6.0 %collective-permute-start.7 = (bf16[400,768]{1,0:T(8,128)(2,1)S(1)}, bf16[400,768]{1,0:T(8,128)(2,1)S(1)}, u32[]{:S(2)}, u32[]{:S(2)}) collective-permute-start(bf16[400,768]{1,0:T(8,128)(2,1)S(1)} %get-tuple-element.48), channel_id=1, source_target_pairs={{31,0},{30,1},{1,2},{0,3},{3,4},{2,5},{5,6},{4,7},{7,8},{6,9},{9,1... | collective-permute-start | bytes 1843208 | tf_op jit(solution)/shard_map/ppermute | solution.py:257
  53.1 6.1 %collective-permute-start.6 = (f32[4,384]{1,0:T(4,128)S(1)}, f32[4,384]{1,0:T(4,128)S(1)}, u32[]{:S(2)}, u32[]{:S(2)}) collective-permute-start(f32[4,384]{1,0:T(4,128)S(1)} %get-tuple-element.46.stat_c), channel_id=1, source_target_pairs={{0,31},{1,30},{2,1},{3,0},{4,3},{5,2},{6,5},{7,4},{8,7},{9,6},{10,... | collective-permute-start | bytes 18440 | tf_op jit(solution)/shard_map/ppermute | solution.py:257
  59.2 2.5 %collective-permute-start.5 = (f32[2,384]{1,0:T(2,128)S(1)}, f32[2,384]{1,0:T(2,128)S(1)}, u32[]{:S(2)}, u32[]{:S(2)}) collective-permute-start(f32[2,384]{1,0:T(2,128)S(1)} %get-tuple-element.47), channel_id=1, source_target_pairs={{0,28},{1,29},{2,30},{3,31},{4,0},{5,1},{6,2},{7,3},{8,4},{9,5},{1... | collective-permute-start | bytes 9224 | tf_op jit(solution)/shard_map/ppermute | solution.py:257
  61.7 3.0 %collective-permute-done.5.from_i = f32[2,384]{1,0:T(2,128)S(1)} collective-permute-done((f32[2,384]{1,0:T(2,128)S(1)}, f32[2,384]{1,0:T(2,128)S(1)}, u32[]{:S(2)}, u32[]{:S(2)}) %collective-permute-start.5) | collective-permute-done | bytes 3104 | tf_op jit(solution)/shard_map/ppermute | solution.py:257
  64.7 8.2 %collective-permute-done.7.home_x = bf16[400,768]{1,0:T(8,128)(2,1)S(1)} collective-permute-done((bf16[400,768]{1,0:T(8,128)(2,1)S(1)}, bf16[400,768]{1,0:T(8,128)(2,1)S(1)}, u32[]{:S(2)}, u32[]{:S(2)}) %collective-permute-start.7) | collective-permute-done | bytes 614432 | tf_op jit(solution)/shard_map/ppermute | solution.py:257
  72.9 1.7 %lse.1 = (bf16[384,768]{1,0:T(8,128)(2,1)}, f32[1,384]{1,0:T(1,128)S(1)}, f32[2,384]{1,0:T(2,128)S(1)}) custom-call(s32[1]{0:T(128)} %bitcast.even, f32[4,384]{1,0:T(4,128)S(1)} %get-tuple-element.46.stat_c, f32[2,384]{1,0:T(2,128)S(1)} %get-tuple-element.43.stat_v, f32[2,384]{1,0:T(2,128)S(1)} %collective-permute-done.5.from_i, ...), custom_call_target="tpu_custom_call" | custom-call | flops 452984832 | tf_op jit(solution)/shard_map/lse/pallas_call | solution.py:262
  74.6 1.9 %collective-permute-start.10 = (bf16[384,768]{1,0:T(8,128)(2,1)}, bf16[384,768]{1,0:T(8,128)(2,1)}, u32[]{:S(2)}, u32[]{:S(2)}) collective-permute-start(bf16[384,768]{1,0:T(8,128)(2,1)} %get-tuple-element.63), channel_id=1, source_target_pairs={{0,1},{1,0},{2,3},{3,2},{4,5},{5,4},{6,7},{7,6},{8,9},{9,8},{10,11... | collective-permute-start | bytes 1769480 | tf_op jit(solution)/shard_map/ppermute | solution.py:257
  76.5 1.4 %text.1 = (f32[384,768]{1,0:T(8,128)S(1)}, f32[384,768]{1,0:T(8,128)S(1)}, f32[1,384]{1,0:T(1,128)S(1)}) custom-call(bf16[384,768]{1,0:T(8,128)(2,1)S(1)} %copy-done.1, f32[1,384]{1,0:T(1,128)S(1)} %get-tuple-element.52.lse_i, f32[2,384]{1,0:T(2,128)S(1)} %get-tuple-element.55.lse_xv, f32[384,384]{1,0:T(8,128)S(1)} %get-tuple-element.53.s_own, ...), custom_call_target="tpu_custom_call" | custom-call | flops 679477248 | tf_op jit(solution)/shard_map/text/pallas_call | solution.py:262
  77.9 3.5 %collective-permute-start.9 = (f32[1,384]{1,0:T(1,128)S(1)}, f32[1,384]{1,0:T(1,128)S(1)}, u32[]{:S(2)}, u32[]{:S(2)}) collective-permute-start(f32[1,384]{1,0:T(1,128)S(1)} %get-tuple-element.59), channel_id=1, source_target_pairs={{0,480},{1,481},{2,482},{3,483},{4,484},{5,485},{6,486},{7,487},{8... | collective-permute-start | bytes 4616 | tf_op jit(solution)/shard_map/ppermute | solution.py:257
  81.5 2.2 %image.1 = (f32[384,768]{1,0:T(8,128)}, f32[1,384]{1,0:T(1,128)S(1)}) custom-call(s32[1]{0:T(128)} %bitcast.even, bf16[384,768]{1,0:T(8,128)(2,1)S(1)} %copy-done.3, f32[1,384]{1,0:T(1,128)S(1)} %get-tuple-element.52.lse_i, f32[384,384]{1,0:T(8,128)S(1)} %get-tuple-element.53.s_own, f32[384,384]{1,0:T(8,128)S(1)} %get-tuple-element.37.s_y, ...), custom_call_target="tpu_custom_call" | custom-call | flops 452984832 | tf_op jit(solution)/shard_map/image/pallas_call | solution.py:262
  84.8 9.5 %collective-permute-done.10.got_p = bf16[384,768]{1,0:T(8,128)(2,1)} collective-permute-done((bf16[384,768]{1,0:T(8,128)(2,1)}, bf16[384,768]{1,0:T(8,128)(2,1)}, u32[]{:S(2)}, u32[]{:S(2)}) %collective-permute-start.10) | collective-permute-done | bytes 589856 | tf_op jit(solution)/shard_map/ppermute | solution.py:257
  94.2 2.2 %last.1 = f32[384,768]{1,0:T(8,128)} custom-call(f32[384,768]{1,0:T(8,128)S(1)} %more.1.text_all, f32[384,768]{1,0:T(8,128)S(1)} %get-tuple-element.62.slope, bf16[384,768]{1,0:T(8,128)(2,1)} %collective-permute-done.10.got_p), custom_call_target="tpu_custom_call" | custom-call | tf_op jit(solution)/shard_map/last/pallas_call | solution.py:262
  (29 shorter events, 3.0 us)
Async XLA Ops:
  0.6 22.0 %collective-permute-start = (bf16[384,768]{1,0:T(8,128)(2,1)}, bf16[384,768]{1,0:T(8,128)(2,1)S(1)}, u32[]{:S(2)}, u32[]{:S(2)}) collective-permute-start(bf16[384,768]{1,0:T(8,128)(2,1)} %pre_txt.3), channel_id=1, source_target_pairs={{0,1},{1,0},{2,3},{3,2},{4,5},{5,4},{6,7},{7,6},{8,9},{9,8},{10,11... | collective-permute-start | bytes 1769480 | tf_op jit(solution)/shard_map/ppermute | solution.py:257
  6.7 27.0 %collective-permute-start.1 = (bf16[384,768]{1,0:T(8,128)(2,1)}, bf16[384,768]{1,0:T(8,128)(2,1)S(1)}, u32[]{:S(2)}, u32[]{:S(2)}) collective-permute-start(bf16[384,768]{1,0:T(8,128)(2,1)} %pre_img.3), channel_id=1, source_target_pairs={{0,28},{1,29},{2,30},{3,31},{4,0},{5,1},{6,2},{7,3},{8,4},{9,5},{1... | collective-permute-start | bytes 1769480 | tf_op jit(solution)/shard_map/ppermute | solution.py:257
  12.1 23.6 %collective-permute-start.2 = (bf16[384,768]{1,0:T(8,128)(2,1)}, bf16[384,768]{1,0:T(8,128)(2,1)S(1)}, u32[]{:S(2)}, u32[]{:S(2)}) collective-permute-start(bf16[384,768]{1,0:T(8,128)(2,1)} %pre_img.3), channel_id=1, source_target_pairs={{0,480},{1,481},{2,482},{3,483},{4,484},{5,485},{6,486},{7,487},{8... | collective-permute-start | bytes 1769480 | tf_op jit(solution)/shard_map/ppermute | solution.py:257
  19.4 1.1 %copy-start = (bf16[384,768]{1,0:T(8,128)(2,1)S(1)}, bf16[384,768]{1,0:T(8,128)(2,1)}, u32[]{:S(2)}) copy-start(bf16[384,768]{1,0:T(8,128)(2,1)} %pre_txt.3) | copy-start | bytes 1769476
  20.4 1.1 %copy-start.2 = (bf16[384,768]{1,0:T(8,128)(2,1)S(1)}, bf16[384,768]{1,0:T(8,128)(2,1)}, u32[]{:S(2)}) copy-start(bf16[384,768]{1,0:T(8,128)(2,1)} %pre_img.3) | copy-start | bytes 1769476
  21.8 23.3 %copy-start.4 = (bf16[384,768]{1,0:T(8,128)(2,1)}, bf16[384,768]{1,0:T(8,128)(2,1)S(1)}, u32[]{:S(2)}) copy-start(bf16[384,768]{1,0:T(8,128)(2,1)S(1)} %get-tuple-element.34.text) | copy-start | bytes 1769476
  22.6 22.6 %collective-permute-start.3 = (bf16[384,768]{1,0:T(8,128)(2,1)S(1)}, bf16[384,768]{1,0:T(8,128)(2,1)S(1)}, u32[]{:S(2)}, u32[]{:S(2)}) collective-permute-start(bf16[384,768]{1,0:T(8,128)(2,1)S(1)} %get-tuple-element.41.image.image_o), channel_id=1, source_target_pairs={{0,31},{1,30},{2,1},{3,0},{4,3},{5,2},{6,5},{7,4},{8,7},{9,6},{10,... | collective-permute-start | bytes 1769480 | tf_op jit(solution)/shard_map/ppermute | solution.py:257
  35.7 26.0 %collective-permute-start.8 = (bf16[400,768]{1,0:T(8,128)(2,1)S(1)}, bf16[400,768]{1,0:T(8,128)(2,1)S(1)}, u32[]{:S(2)}, u32[]{:S(2)}) collective-permute-start(bf16[400,768]{1,0:T(8,128)(2,1)S(1)} %get-tuple-element.49), channel_id=1, source_target_pairs={{28,0},{29,1},{30,2},{31,3},{0,4},{1,5},{2,6},{3,7},{4,8},{5,9},{6... | collective-permute-start | bytes 1843208 | tf_op jit(solution)/shard_map/ppermute | solution.py:257
  39.3 0.8 copy-start.6
  40.1 6.9 %copy-start.8 = (f32[384,384]{1,0:T(8,128)}, f32[384,384]{1,0:T(8,128)S(1)}, u32[]{:S(2)}) copy-start(f32[384,384]{1,0:T(8,128)S(1)} %get-tuple-element.60.s_h) | copy-start | bytes 1769476
  40.1 12.9 %collective-permute-start.4 = (bf16[400,768]{1,0:T(8,128)(2,1)S(1)}, bf16[400,768]{1,0:T(8,128)(2,1)S(1)}, u32[]{:S(2)}, u32[]{:S(2)}) collective-permute-start(bf16[400,768]{1,0:T(8,128)(2,1)S(1)} %get-tuple-element.45), channel_id=1, source_target_pairs={{480,0},{481,1},{482,2},{483,3},{484,4},{485,5},{486,6},{487,7},{4... | collective-permute-start | bytes 1843208 | tf_op jit(solution)/shard_map/ppermute | solution.py:257
  47.1 25.9 %collective-permute-start.7 = (bf16[400,768]{1,0:T(8,128)(2,1)S(1)}, bf16[400,768]{1,0:T(8,128)(2,1)S(1)}, u32[]{:S(2)}, u32[]{:S(2)}) collective-permute-start(bf16[400,768]{1,0:T(8,128)(2,1)S(1)} %get-tuple-element.48), channel_id=1, source_target_pairs={{31,0},{30,1},{1,2},{0,3},{3,4},{2,5},{5,6},{4,7},{7,8},{6,9},{9,1... | collective-permute-start | bytes 1843208 | tf_op jit(solution)/shard_map/ppermute | solution.py:257
  53.1 11.6 %collective-permute-start.6 = (f32[4,384]{1,0:T(4,128)S(1)}, f32[4,384]{1,0:T(4,128)S(1)}, u32[]{:S(2)}, u32[]{:S(2)}) collective-permute-start(f32[4,384]{1,0:T(4,128)S(1)} %get-tuple-element.46.stat_c), channel_id=1, source_target_pairs={{0,31},{1,30},{2,1},{3,0},{4,3},{5,2},{6,5},{7,4},{8,7},{9,6},{10,... | collective-permute-start | bytes 18440 | tf_op jit(solution)/shard_map/ppermute | solution.py:257
  59.2 5.5 %collective-permute-start.5 = (f32[2,384]{1,0:T(2,128)S(1)}, f32[2,384]{1,0:T(2,128)S(1)}, u32[]{:S(2)}, u32[]{:S(2)}) collective-permute-start(f32[2,384]{1,0:T(2,128)S(1)} %get-tuple-element.47), channel_id=1, source_target_pairs={{0,28},{1,29},{2,30},{3,31},{4,0},{5,1},{6,2},{7,3},{8,4},{9,5},{1... | collective-permute-start | bytes 9224 | tf_op jit(solution)/shard_map/ppermute | solution.py:257
  72.9 3.6 %copy-start.1 = (bf16[384,768]{1,0:T(8,128)(2,1)S(1)}, bf16[384,768]{1,0:T(8,128)(2,1)}, u32[]{:S(2)}) copy-start(bf16[384,768]{1,0:T(8,128)(2,1)} %pre_txt.3) | copy-start | bytes 1769476
  74.6 19.6 %collective-permute-start.10 = (bf16[384,768]{1,0:T(8,128)(2,1)}, bf16[384,768]{1,0:T(8,128)(2,1)}, u32[]{:S(2)}, u32[]{:S(2)}) collective-permute-start(bf16[384,768]{1,0:T(8,128)(2,1)} %get-tuple-element.63), channel_id=1, source_target_pairs={{0,1},{1,0},{2,3},{3,2},{4,5},{5,4},{6,7},{7,6},{8,9},{9,8},{10,11... | collective-permute-start | bytes 1769480 | tf_op jit(solution)/shard_map/ppermute | solution.py:257
  76.5 4.9 %copy-start.3 = (bf16[384,768]{1,0:T(8,128)(2,1)S(1)}, bf16[384,768]{1,0:T(8,128)(2,1)}, u32[]{:S(2)}) copy-start(bf16[384,768]{1,0:T(8,128)(2,1)} %pre_img.3) | copy-start | bytes 1769476
  76.5 4.9 %copy-start.5 = (bf16[384,768]{1,0:T(8,128)(2,1)S(1)}, bf16[384,768]{1,0:T(8,128)(2,1)}, u32[]{:S(2)}) copy-start(bf16[384,768]{1,0:T(8,128)(2,1)} %copy-done.4) | copy-start | bytes 1769476
  77.9 6.4 %copy-start.7 = (bf16[384,768]{1,0:T(8,128)(2,1)S(1)}, bf16[384,768]{1,0:T(8,128)(2,1)}, u32[]{:S(2)}) copy-start(bf16[384,768]{1,0:T(8,128)(2,1)} %copy-done.6) | copy-start | bytes 1769476
  77.9 6.4 %copy-start.9 = (f32[384,384]{1,0:T(8,128)S(1)}, f32[384,384]{1,0:T(8,128)}, u32[]{:S(2)}) copy-start(f32[384,384]{1,0:T(8,128)} %copy-done.8) | copy-start | bytes 1769476
  77.9 6.4 %collective-permute-start.9 = (f32[1,384]{1,0:T(1,128)S(1)}, f32[1,384]{1,0:T(1,128)S(1)}, u32[]{:S(2)}, u32[]{:S(2)}) collective-permute-start(f32[1,384]{1,0:T(1,128)S(1)} %get-tuple-element.59), channel_id=1, source_target_pairs={{0,480},{1,481},{2,482},{3,483},{4,484},{5,485},{6,486},{7,487},{8... | collective-permute-start | bytes 4616 | tf_op jit(solution)/shard_map/ppermute | solution.py:257
